TPU v7x, 256 devices: a whole 4x4x8 slice. The times are simulated.
256 devices in a mesh: dp: 64 (over z, x, core), seq: 4 (over y).
Axes of the slice: x: 4, y: 4, z: 8, core: 2. Of those that a mesh axis runs over, the one named last changes fastest.
Arguments:
- qkv: bfloat16 [64, 1024, 4608], P('dp', 'seq'), may hold values from -7 to 7
- grad_in: bfloat16 [64, 256, 4, 1536], P('dp', 'seq'), may hold values from -6 to 6
- counts: int32 [64, 256], P('dp', 'seq'), may hold values from 1 to 4
- segment: int32 [64, 1024], P('dp', 'seq'), may hold values from 0 to 3, never falling along the last dimension, each value on 1 to 512 neighbouring positions
- conv_weight: float32 [31, 1536], replicated, may hold values from -1 to 1
Outputs:
- qkv_grad: bfloat16 [64, 256, 4, 4608], P('dp', 'seq')
- conv_weight_grad: float32 [31, 1536], replicated
Inputs may be any that keep to these rules, and one draw needn't show every extreme that they name: `segment`: never falls along time within an owner's recording; each utterance has 1 to 512 frame slots, one exactly that many.
All inputs are finite; a program needn't handle non-finite values.
Results may differ from a plain program's by a relative error of at most 0.025.
Values may be sent and summed in bfloat16 or wider, within the bound.
A program may use at most 128 MiB of HBM per device.

v0:
```python
import math

import jax
import jax.numpy as jnp
from jax import lax
from jax.sharding import PartitionSpec as P

H = 16


masked_score = -1e30
heads_per_group = 4


def padded(block, sides, width):
    for axis, dim in sides:
        count = lax.axis_size(axis)
        forward = [(i, i + 1) for i in range(count - 1)]
        backward = [(target, source) for source, target in forward]
        low = lax.ppermute(
            lax.slice_in_dim(block, block.shape[dim] - width, None, axis=dim), axis, forward
        )
        high = lax.ppermute(lax.slice_in_dim(block, 0, width, axis=dim), axis, backward)
        block = jnp.concatenate([low, block, high], axis=dim)
    return block


def local(qkv, grad_in, counts, segment, conv_weight):
    data_size = lax.axis_size("dp")
    time_size = lax.axis_size("seq")
    rows_here = qkv.shape[1]
    width = qkv.shape[2] // 3
    slot_rows = grad_in.shape[2]
    taps = conv_weight.shape[0]
    margin = (taps - 1) // 2
    head_count = H
    head_size = width // head_count
    group_count = head_count // heads_per_group
    time_rows = rows_here * time_size
    score_scale = head_size ** (-0.5)

    def by_group(values):
        length = values.shape[0]
        return values.reshape(length, group_count, heads_per_group, head_size).transpose(1, 0, 2, 3)

    def from_group(values):
        length = values.shape[1]
        return values.transpose(1, 0, 2, 3).reshape(length, width)

    arrived, got_counts = (
        lax.all_to_all(grad_in, "dp", split_axis=1, concat_axis=0, tiled=True),
        lax.all_to_all(counts, "dp", split_axis=1, concat_axis=0, tiled=True),
    )
    filled = (jnp.arange(slot_rows)[None, :] < got_counts).reshape(rows_here)
    seg_own = segment[0]
    labels = jnp.where(filled, seg_own + 1, 0)
    cotangent = jnp.where(
        filled[:, None], arrived.reshape(rows_here, width), jnp.zeros((), jnp.bfloat16)
    )
    queries = qkv[0, :, :width]
    keyvals = qkv[0, :, width:]
    label_wire = labels.astype(jnp.bfloat16)
    all_kv, all_label = (
        lax.all_gather(keyvals, "seq", axis=0, tiled=True),
        lax.all_gather(label_wire, "seq", axis=0, tiled=True),
    )
    own_pos = lax.axis_index("seq") * rows_here + jnp.arange(rows_here)
    time_index = jnp.arange(time_rows)
    allowed = (all_label.astype(jnp.int32)[None, :] == seg_own[:, None] + 1) | (
        own_pos[:, None] == time_index[None, :]
    )
    query_groups = by_group(queries)
    key_groups = by_group(all_kv[:, :width])
    value_groups = by_group(all_kv[:, width:])

    def forward(inputs):
        queries_in, keys_in, values_in = inputs
        scores = (
            jnp.einsum("rhd,uhd->hru", queries_in, keys_in, preferred_element_type=jnp.float32)
            * score_scale
        )
        scores = jnp.where(allowed[None], scores, masked_score)
        highest = jnp.max(scores, -1, keepdims=True)
        row_total = jnp.sum(
            jnp.where(allowed[None], jnp.exp(scores - highest), 0.0), -1, keepdims=True
        )
        log_total = highest + jnp.log(row_total)
        soft_rounded = jnp.where(allowed[None], jnp.exp(scores - log_total), 0.0).astype(
            jnp.bfloat16
        )
        result = jnp.einsum(
            "hru,uhd->rhd", soft_rounded, values_in, preferred_element_type=jnp.float32
        )
        return (result.astype(jnp.bfloat16), log_total[..., 0])

    out_groups, log_groups = lax.map(forward, (query_groups, key_groups, value_groups))
    attended = from_group(out_groups)
    pad_att, pad_cot, pad_wire = (
        padded(attended, (("seq", 0),), margin),
        padded(cotangent, (("seq", 0),), margin),
        padded(label_wire, (("seq", 0),), margin),
    )
    pad_lab = pad_wire.astype(jnp.int32)
    own_ok = labels > 0
    cot_wide = cotangent.astype(jnp.float32)

    def tap_step(tap_index, state_pair):
        grad_att, grad_taps = state_pair
        cot_in = lax.dynamic_slice_in_dim(pad_cot, 2 * margin - tap_index, rows_here, 0)
        lab_near = lax.dynamic_slice_in_dim(pad_lab, 2 * margin - tap_index, rows_here, 0)
        near = (lab_near == labels) & own_ok
        weight_row = lax.dynamic_index_in_dim(conv_weight, tap_index, 0, keepdims=False)
        grad_att = grad_att + weight_row[None, :] * jnp.where(
            near[:, None], cot_in.astype(jnp.float32), 0.0
        )
        att_in = lax.dynamic_slice_in_dim(pad_att, tap_index, rows_here, 0)
        lab_close = lax.dynamic_slice_in_dim(pad_lab, tap_index, rows_here, 0)
        close = (lab_close == labels) & own_ok
        term = jnp.sum(jnp.where(close[:, None], cot_wide * att_in.astype(jnp.float32), 0.0), 0)
        grad_taps = lax.dynamic_update_index_in_dim(grad_taps, term, tap_index, 0)
        return (grad_att, grad_taps)

    start_pair = (jnp.zeros((rows_here, width), jnp.float32), jnp.zeros((taps, width), jnp.float32))
    attended_grad, tap_terms = lax.fori_loop(0, taps, tap_step, start_pair)
    tap_total = lax.psum(tap_terms, ("dp", "seq"))
    conv_weight_grad = tap_total / math.sqrt(data_size * slot_rows)
    dout = attended_grad.astype(jnp.bfloat16)
    delta = jnp.sum(
        (dout.astype(jnp.float32) * attended.astype(jnp.float32)).reshape(
            rows_here, head_count, head_size
        ),
        -1,
    )
    dout_groups = by_group(dout)
    length = delta.shape[0]
    delta_groups = delta.reshape(length, group_count, heads_per_group).transpose(1, 2, 0)

    def gradients(queries_in, keys_in, values_in, dout_in, log_in, delta_in, permit):
        scores = (
            jnp.einsum("rhd,uhd->hru", queries_in, keys_in, preferred_element_type=jnp.float32)
            * score_scale
        )
        scores = jnp.where(permit[None], scores, masked_score)
        soft_weights = jnp.where(permit[None], jnp.exp(scores - log_in[..., None]), 0.0)
        soft_rounded = soft_weights.astype(jnp.bfloat16)
        value_grad = jnp.einsum(
            "hru,rhd->uhd", soft_rounded, dout_in, preferred_element_type=jnp.float32
        )
        prob_grad = jnp.einsum(
            "rhd,uhd->hru", dout_in, values_in, preferred_element_type=jnp.float32
        )
        score_grad = (soft_weights * (prob_grad - delta_in[..., None]) * score_scale).astype(
            jnp.bfloat16
        )
        query_grad = jnp.einsum(
            "hru,uhd->rhd", score_grad, keys_in, preferred_element_type=jnp.float32
        )
        key_grad = jnp.einsum(
            "hru,rhd->uhd", score_grad, queries_in, preferred_element_type=jnp.float32
        )
        return (query_grad, key_grad, value_grad)

    def own_queries(inputs):
        return gradients(inputs[0], inputs[1], inputs[2], inputs[3], inputs[4], inputs[5], allowed)

    dq_groups, dk_groups, dv_groups = lax.map(
        own_queries, (query_groups, key_groups, value_groups, dout_groups, log_groups, delta_groups)
    )
    query_grad = from_group(dq_groups).astype(jnp.bfloat16)
    key_terms = jnp.concatenate([from_group(dk_groups), from_group(dv_groups)], 1)
    key_grads = lax.psum_scatter(
        key_terms.astype(jnp.bfloat16), "seq", scatter_dimension=0, tiled=True
    )
    owned = jnp.concatenate([query_grad, key_grads], 1)
    qkv_grad = lax.all_to_all(
        owned.reshape(data_size, 1, slot_rows, 3 * width),
        "dp",
        split_axis=0,
        concat_axis=1,
        tiled=True,
    )
    return (qkv_grad, conv_weight_grad)


def solution(mesh):
    in_specs = (
        P("dp", "seq", None),
        P("dp", "seq", None, None),
        P("dp", "seq"),
        P("dp", "seq"),
        P(),
    )
    out_specs = (P("dp", "seq", None, None), P())
    return jax.shard_map(local, mesh=mesh, in_specs=in_specs, out_specs=out_specs, check_vma=False)
```

profile of v0, /device:TPU:1, one launch (start us, length us, event | category | flops | bytes accessed | tf_op | source)
XLA Modules:
  0.0 803.8 jit_solution(6869868235228481976)
XLA Ops:
  10.0 22.3 %all_to_all.34 = s32[1,64,1]{2,0,1:T(1,128)S(1)} all-to-all(s32[1,64,1]{2,0,1:T(1,128)S(1)} %copy.38), channel_id=1, replica_groups=mesh['dp'=64,'seq'=4] {'dp'}, dimensions={1} | all-to-all | bytes 512 | tf_op jit(solution)/shard_map/all_to_all | solution.py:52
  32.3 4.8 all-to-all-start.1
  39.8 8.8 %all-gather.1 = bf16[4,1,256]{2,1,0:T(2,128)(2,1)S(1)} all-gather(bf16[1,1,256]{2,1,0:T(2,128)(2,1)S(1)} %reshape.130), channel_id=1, replica_groups=mesh['dp'=64,'seq'=4] {'seq'}, dimensions={0}, use_global_device_ids=true | all-gather | bytes 2560 | tf_op jit(solution)/shard_map/all_gather | solution.py:65
  54.7 5.3 all-to-all-done.1
  67.0 16.2 %all-gather.4.cloned.1.call-done = bf16[1,1024,3072]{2,1,0:T(8,128)(2,1)} async-done(((bf16[1,256,3072]{2,1,0:T(8,128)(2,1)}), bf16[1,1024,3072]{2,1,0:T(8,128)(2,1)}) %all-gather.4.cloned.1.call-update) | async-done | bytes 6291472 | tf_op jit(solution)/shard_map/all_gather | solution.py:64
  83.2 5.8 fusion.55
  92.3 4.7 copy.37
  96.9 27.9 %while.46 = (s32[]{:T(128)}, bf16[4,256,4,96]{1,3,2,0:T(8,128)(2,1)}, f32[4,4,256]{2,1,0:T(4,128)S(1)}, bf16[4,1024,4,96]{1,3,2,0:T(8,128)(2,1)}, bf16[4,256,4,9...) while((s32[]{:T(128)}, ...), condition=%wide.region_3.4_spmd.clone, body=%wide.region_0.3_spmd.clone.sunk | while | flops 417168384 | bytes 15638633 | solution.py:96
  133.8 3.9 collective-permute-done.4
  137.7 3.8 collective-permute-done.5
  143.2 241.6 %while.48 = (s32[]{:T(128)}, f32[256,1536]{1,0:T(8,128)}, f32[31,1536]{1,0:T(8,128)}, f32[31,1536]{1,0:T(8,128)}, s32[286]{0:T(512)S(1)}, /*index=5*/s32[256]{0:...) while((s32[]{:T(128)}, f32[256,1536]{1,0:T(8,128)}, ...), condition=%wide.region_6.7_spmd.clone, body=%wide.region_4.6_spmd.clone.sunk | while | flops 3538439 | bytes 15782385 | solution.py:124
  153.5 3.4 select_add_fusion.2
  161.3 3.4 select_add_fusion.2
  169.1 3.4 select_add_fusion.2
  176.9 3.4 select_add_fusion.2
  184.8 3.4 select_add_fusion.2
  192.6 3.4 select_add_fusion.2
  200.4 3.4 select_add_fusion.2
  208.2 3.4 select_add_fusion.2
  216.0 3.4 select_add_fusion.2
  223.8 3.4 select_add_fusion.2
  231.6 3.4 select_add_fusion.2
  239.4 3.4 select_add_fusion.2
  247.2 3.4 select_add_fusion.2
  255.0 3.4 select_add_fusion.2
  262.9 3.4 select_add_fusion.2
  270.7 3.4 select_add_fusion.2
  278.5 3.4 select_add_fusion.2
  286.3 3.4 select_add_fusion.2
  294.1 3.4 select_add_fusion.2
  301.9 3.4 select_add_fusion.2
  309.7 3.4 select_add_fusion.2
  317.5 3.4 select_add_fusion.2
  325.3 3.4 select_add_fusion.2
  333.1 3.4 select_add_fusion.2
  341.0 3.4 select_add_fusion.2
  348.8 3.4 select_add_fusion.2
  356.6 3.4 select_add_fusion.2
  391.9 48.2 %while.47 = (s32[]{:T(128)}, bf16[4,256,4,96]{1,3,2,0:T(8,128)(2,1)}, bf16[4,1024,4,96]{1,3,2,0:T(8,128)(2,1)}, bf16[4,1024,4,96]{1,3,2,0:T(8,128)(2,1)}, bf16[4...) while((s32[]{:T(128)}, ...), condition=%wide.region_9.10_spmd.clone, body=%wide.region_8.9_spmd.clone.sunk | while | flops 1021050880 | bytes 79863056 | solution.py:166
  394.0 3.5 multiply_convert_fusion.2
  406.0 3.5 multiply_convert_fusion.2
  418.1 3.5 multiply_convert_fusion.2
  430.1 3.5 multiply_convert_fusion.2
  443.3 4.7 copy.43
  448.0 5.3 pad_maximum_fusion
  454.7 66.3 %reduce-scatter.2.cloned.1.call-done = bf16[256,3072]{1,0:T(8,128)(2,1)} async-done(((bf16[1024,3072]{1,0:T(8,128)(2,1)}), bf16[256,3072]{1,0:T(8,128)(2,1)}) %reduce-scatter.2.cloned.1.call-update) | async-done | bytes 1572880 | tf_op jit(solution)/shard_map/reduce_scatter | solution.py:171
  524.7 10.6 %all-to-all-start.2 = ((bf16[64,1,4,4608]{3,2,1,0:T(4,128)(2,1)}), bf16[64,1,4,4608]{3,2,1,0:T(4,128)(2,1)S(1)}, u32[]{:S(2)}, u32[]{:S(2)}) async-start(bf16[64,1,4,4608]{3,2,1,0:T(4,128)(2,1)} %reshape.128), calls=%async_computation.3 | async-start | bytes 4718592 | tf_op jit(solution)/shard_map/all_to_all | solution.py:175
  536.0 258.2 %all-reduce.2.cloned.1.call-done = f32[31,1536]{1,0:T(8,128)} async-done(((f32[31,1536]{1,0:T(8,128)}), f32[31,1536]{1,0:T(8,128)}) %all-reduce.2.cloned.1.call-update) | async-done | bytes 190480 | tf_op jit(solution)/shard_map/psum | solution.py:125
  (405 shorter events, 261.3 us)
Async XLA Ops:
  7.2 76.1 %all-gather.4.cloned.1.call-start = ((), (), s32[]{:S(2)}) async-start(), calls=%async_computation.6 | async-start | bytes 7864320 | tf_op jit(solution)/shard_map/all_gather | solution.py:64
  9.9 27.3 %slice-start = ((bf16[1,256,4608]{2,1,0:T(8,128)(2,1)}), bf16[1,256,1536]{2,1,0:T(8,128)(2,1)S(1)}, s32[]{:S(2)}) async-start(bf16[1,256,4608]{2,1,0:T(8,128)(2,1)} %param.11), calls=%async_computation.7 | async-start | bytes 1572864 | tf_op jit(solution)/shard_map/slice | solution.py:60
  9.9 28.5 %copy-start.10 = (s32[1,256]{1,0:T(1,128)S(1)}, s32[1,256]{1,0:T(1,128)}, u32[]{:S(2)}) copy-start(s32[1,256]{1,0:T(1,128)} %param.14) | copy-start | bytes 3076
  32.3 27.8 %all-to-all-start.1 = ((bf16[1,64,4,1536]{3,2,0,1:T(4,128)(2,1)}), bf16[1,64,4,1536]{3,2,0,1:T(4,128)(2,1)S(1)}, u32[]{:S(2)}, u32[]{:S(2)}) async-start(bf16[1,64,4,1536]{3,2,0,1:T(4,128)(2,1)} %bitcast.12), calls=%async_computation.1 | async-start | bytes 1572864 | tf_op jit(solution)/shard_map/all_to_all | solution.py:51
  37.1 483.9 %reduce-scatter.2.cloned.1.call-start = ((), (), s32[]{:S(2)}) async-start(), calls=%async_computation.4 | async-start | bytes 7864320 | tf_op jit(solution)/shard_map/reduce_scatter | solution.py:171
  48.7 2.6 collective-permute-start
  50.0 4.7 collective-permute-start.1
  62.5 68.9 %collective-permute-start.2 = (bf16[15,1536]{1,0:T(8,128)(2,1)S(1)}, bf16[15,1536]{1,0:T(8,128)(2,1)S(1)}, u32[]{:S(2)}, u32[]{:S(2)}) collective-permute-start(bf16[15,1536]{1,0:T(8,128)(2,1)S(1)} %get-tuple-element.548), channel_id=1, source_target_pairs={{0,1},{1,2},{2,3},{4,5},{5,6},{6,7},{8,9},{9,10},{10,11},{12,13},{... | collective-permute-start | bytes 138248 | tf_op jit(solution)/shard_map/ppermute | solution.py:20
  65.7 65.7 %collective-permute-start.3 = (bf16[15,1536]{1,0:T(8,128)(2,1)S(1)}, bf16[15,1536]{1,0:T(8,128)(2,1)S(1)}, u32[]{:S(2)}, u32[]{:S(2)}) collective-permute-start(bf16[15,1536]{1,0:T(8,128)(2,1)S(1)} %get-tuple-element.549), channel_id=1, source_target_pairs={{1,0},{2,1},{3,2},{5,4},{6,5},{7,6},{9,8},{10,9},{11,10},{13,12},{... | collective-permute-start | bytes 138248 | tf_op jit(solution)/shard_map/ppermute | solution.py:23
  124.8 18.4 %copy-start = (bf16[4,1024,4,96]{1,3,2,0:T(8,128)(2,1)}, bf16[4,1024,4,96]{1,3,2,0:T(8,128)(2,1)S(1)}, u32[]{:S(2)}) copy-start(bf16[4,1024,4,96]{1,3,2,0:T(8,128)(2,1)S(1)} %get-tuple-element.888) | copy-start | bytes 9437188
  124.8 16.7 %copy-start.3 = (bf16[4,256,4,96]{1,3,2,0:T(8,128)(2,1)S(1)}, bf16[4,256,4,96]{1,3,2,0:T(8,128)(2,1)}, u32[]{:S(2)}) copy-start(bf16[4,256,4,96]{1,3,2,0:T(8,128)(2,1)} %get-tuple-element.343) | copy-start | bytes 2359300
  126.8 10.9 %collective-permute-start.4 = (bf16[15,1536]{0,1:T(8,128)(2,1)S(1)}, bf16[15,1536]{0,1:T(8,128)(2,1)S(1)}, u32[]{:S(2)}, u32[]{:S(2)}) collective-permute-start(bf16[15,1536]{0,1:T(8,128)(2,1)S(1)} %bitcast.147), channel_id=1, source_target_pairs={{0,1},{1,2},{2,3},{4,5},{5,6},{6,7},{8,9},{9,10},{10,11},{12,13},{... | collective-permute-start | bytes 138248 | tf_op jit(solution)/shard_map/ppermute | solution.py:20
  129.9 11.6 %collective-permute-start.5 = (bf16[15,1536]{0,1:T(8,128)(2,1)S(1)}, bf16[15,1536]{0,1:T(8,128)(2,1)S(1)}, u32[]{:S(2)}, u32[]{:S(2)}) collective-permute-start(bf16[15,1536]{0,1:T(8,128)(2,1)S(1)} %bitcast.146), channel_id=1, source_target_pairs={{1,0},{2,1},{3,2},{5,4},{6,5},{7,6},{9,8},{10,9},{11,10},{13,12},{... | collective-permute-start | bytes 138248 | tf_op jit(solution)/shard_map/ppermute | solution.py:23
  143.3 2.8 copy-start.2
  150.7 2.8 copy-start.2
  158.5 2.8 copy-start.2
  166.3 2.8 copy-start.2
  174.1 2.8 copy-start.2
  181.9 2.8 copy-start.2
  189.7 2.8 copy-start.2
  197.5 2.8 copy-start.2
  205.3 2.8 copy-start.2
  213.1 2.8 copy-start.2
  221.0 2.8 copy-start.2
  228.8 2.8 copy-start.2
  236.6 2.8 copy-start.2
  244.4 2.8 copy-start.2
  252.2 2.8 copy-start.2
  260.0 2.8 copy-start.2
  267.8 2.8 copy-start.2
  275.6 2.8 copy-start.2
  283.4 2.8 copy-start.2
  291.2 2.8 copy-start.2
  299.1 2.8 copy-start.2
  306.9 2.8 copy-start.2
  314.7 2.8 copy-start.2
  322.5 2.8 copy-start.2
  330.3 2.8 copy-start.2
  338.1 2.8 copy-start.2
  345.9 2.8 copy-start.2
  353.7 2.8 copy-start.2
  384.9 7.0 copy-start.1
  394.0 3.6 copy-start.5
  406.0 3.6 copy-start.5
  418.1 3.5 copy-start.5
  430.1 3.6 copy-start.5
  524.7 271.2 %all-to-all-start.2 = ((bf16[64,1,4,4608]{3,2,1,0:T(4,128)(2,1)}), bf16[64,1,4,4608]{3,2,1,0:T(4,128)(2,1)S(1)}, u32[]{:S(2)}, u32[]{:S(2)}) async-start(bf16[64,1,4,4608]{3,2,1,0:T(4,128)(2,1)} %reshape.128), calls=%async_computation.3 | async-start | bytes 4718592 | tf_op jit(solution)/shard_map/all_to_all | solution.py:175
  535.3 259.0 %all-reduce.2.cloned.1.call-start = ((), (), s32[]{:S(2)}) async-start(), calls=%async_computation.5 | async-start | bytes 393216 | tf_op jit(solution)/shard_map/psum | solution.py:125
  (21 other events, 41.9 us)
Sparse Core Ops, SparseCore 0:
  10.4 72.8 all-gather.3
  453.4 67.5 reduce-scatter.1
  542.2 252.0 all-reduce.1
where the time goes:
time: 811 us; the launch traced here: 804 us
  waiting for transfers between devices  358 us (44%)
  local copies, waits for them, and re-layouts  177 us (22%)
  other arithmetic  136 us (17%)
  matrix products  59.3 us (7%)
  blocking collectives  31.1 us (4%)
  starting transfers between devices  27.2 us (3%)
  between operations  14 us (2%)
    psum x1, waiting for transfers between devices, local(): tap_total = lax.psum(tap_terms, ('dp', 'seq'))  258 us
    add x31, other arithmetic, tap_step(): grad_att + weight_row[None, :] * jnp.where(near[:, None], cot_in.astype(j...  106 us
    reduce_scatter x1, waiting for transfers between devices, local(): lax.psum_scatter(key_terms.astype(jnp.bfloat16), 'seq', scatter_dimension...  66.3 us
    dynamic_slice x62, local copies, waits for them, and re-layouts, tap_step(): att_in = lax.dynamic_slice_in_dim(pad_att, tap_index, rows_here, 0)  61.9 us
    dynamic_update_slice x31, local copies, waits for them, and re-layouts, tap_step(): grad_taps = lax.dynamic_update_index_in_dim(grad_taps, term, tap_index, 0)  44.7 us
    dynamic_slice x31, local copies, waits for them, and re-layouts, tap_step(): lax.dynamic_index_in_dim(conv_weight, tap_index, 0, keepdims=False)  25.7 us
    all_to_all x1, blocking collectives, local(): lax.all_to_all(counts, 'dp', split_axis=1, concat_axis=0, tiled=True)  22.3 us
    all_gather x1, waiting for transfers between devices, local(): lax.all_gather(keyvals, 'seq', axis=0, tiled=True)  16.2 us
  transfers between devices with their start and end apart: 11, of which 7 were waited for; matrix products, arithmetic and copies ran while one was open for 7% of the time, Pallas kernels for 0%

commit v1 on v0

v1 whole, which is shorter than its diff:
```python
import functools
import math

import jax
import jax.numpy as jnp
from jax import lax
from jax.experimental import pallas as pl
from jax.experimental.pallas import tpu as pltpu
from jax.sharding import PartitionSpec as P

H = 16

EMPTY = 128.0
EMPTY_ABOVE = 64.0
MASKED = -1e30
LANES = 128
TB = 256
UB = 128
GAP = 16
CH = 128


def dot(a, b, contract):
    return lax.dot_general(a, b, (contract, ((), ())), preferred_element_type=jnp.float32)


def block_kernel(
    time_rows,
    width,
    head_size,
    taps,
    bounds_ref,
    qkv_ref,
    cot_ref,
    seg_ref,
    cw_ref,
    out_ref,
    taps_ref,
    segb,
    labb,
    shifted,
    grad_pad,
    att_pad,
    k_t,
    v_t,
    do_t,
    att_t,
    dq_t,
    dk,
    dv,
    scores,
    probs,
):
    f32, bf16 = jnp.float32, jnp.bfloat16
    margin = (taps - 1) // 2
    heads = width // head_size
    tiles = width // LANES
    scale = head_size ** (-0.5)
    seg_count = 4
    inner = time_rows + GAP * (seg_count - 1)
    rows_all = shifted.shape[1]

    def rows(index, size):
        return pl.ds(pl.multiple_of(index * size, size), size)

    def chunks(count, body):
        def step(index, carry):
            body(index)
            return carry

        lax.fori_loop(0, count, step, 0)

    def make_labels(c):
        here = rows(c, CH)
        across = jnp.broadcast_to(seg_ref[:, here], (CH, CH)).T
        segb[here, :] = across
        got = cot_ref[here, :LANES].astype(f32)
        labb[here, :] = jnp.where(got < EMPTY_ABOVE, across + 1.0, 0.0)

    chunks(time_rows // CH, make_labels)

    def clear(c):
        here = rows(c, 8)
        shifted[0, here, :] = jnp.zeros((8, width), f32)
        att_pad[here, :] = jnp.zeros((8, width), f32)

    chunks(rows_all // 8, clear)

    def spread(c):
        here = rows(c, CH)
        lab = labb[here, :]
        for j in range(tiles):
            cols = pl.ds(j * LANES, LANES)
            val = cot_ref[here, cols].astype(f32)
            for s in range(seg_count):
                there = pl.ds(pl.multiple_of(c * CH + GAP * (s + 1), GAP), CH)
                shifted[0, there, cols] += jnp.where(lab == s + 1.0, val, 0.0)

    chunks(time_rows // CH, spread)

    def shift(c):
        r0 = pl.multiple_of(c * 48, 8)
        for j in range(tiles):
            cols = pl.ds(j * LANES, LANES)
            block = shifted[0, pl.ds(r0, 56), cols]
            for b in range(1, 8):
                shifted[b, pl.ds(r0, 48), cols] = block[b : b + 48]

    chunks((rows_all - 8) // 48, shift)

    def tap_view(w, r0, size, cols):
        offset = margin - w
        a, b = offset // 8, offset % 8
        return shifted[b, pl.ds(pl.multiple_of(r0 + GAP + 8 * a, 8), size), cols]

    def conv(c):
        r0 = c * 32
        for j in range(tiles):
            cols = pl.ds(j * LANES, LANES)
            total = jnp.zeros((32, LANES), f32)
            for w in range(taps):
                total = total + cw_ref[w : w + 1, cols] * tap_view(w, r0, 32, cols)
            grad_pad[pl.ds(pl.multiple_of(r0, 16), 32), cols] = total

    chunks(grad_pad.shape[0] // 32, conv)

    def transposes(c):
        here = rows(c, CH)
        lab = labb[here, :]
        for j in range(tiles):
            cols = pl.ds(j * LANES, LANES)
            total = jnp.zeros((CH, LANES), f32)
            for s in range(seg_count):
                there = pl.ds(pl.multiple_of(c * CH + GAP * s, GAP), CH)
                total = total + jnp.where(lab == s + 1.0, grad_pad[there, cols], 0.0)
            do_t[cols, here] = total.T
            k_t[cols, here] = qkv_ref[here, pl.ds(width + j * LANES, LANES)].astype(f32).T.astype(bf16)
            v_t[cols, here] = qkv_ref[here, pl.ds(2 * width + j * LANES, LANES)].astype(f32).T.astype(bf16)
        dk[here, :] = jnp.zeros((CH, width), f32)
        dv[here, :] = jnp.zeros((CH, width), f32)

    chunks(time_rows // CH, transposes)

    row_index = lax.broadcasted_iota(jnp.int32, (UB, TB), 0)
    col_index = lax.broadcasted_iota(jnp.int32, (UB, TB), 1)
    apart = col_index - row_index
    to_exp2 = scale * math.log2(math.e)

    for h in range(heads):
        first, last = h * head_size, (h + 1) * head_size
        lane0 = first // LANES * LANES
        span = -(-last // LANES) * LANES - lane0
        before, after = first - lane0, lane0 + span - last
        head_rows = pl.ds(first, head_size)
        lane = lax.broadcasted_iota(jnp.int32, (TB, span), 1)
        in_head = (lane >= before) & (lane < before + head_size)

        def time_block(tb, carry):
            here = rows(tb, TB)
            low, high = bounds_ref[tb, 0], bounds_ref[tb, 1]
            q = jnp.where(in_head, qkv_ref[here, pl.ds(lane0, span)], jnp.zeros((), bf16))
            want = seg_ref[:, here] + 1.0

            def score_step(ub, highest):
                keys = rows(ub, UB)
                s = dot(qkv_ref[keys, pl.ds(width + lane0, span)], q, ((1,), (1,)))
                lab = labb[keys, :]
                lab = jnp.concatenate([lab] * (TB // LANES), axis=1)
                ok = (lab == want) | (apart == ub * UB - tb * TB)
                s = jnp.where(ok, s, MASKED)
                scores[keys, :] = s
                return jnp.maximum(highest, jnp.max(s.reshape(UB // 8, 8, TB), axis=0))

            highest = lax.fori_loop(low, high, score_step, jnp.full((8, TB), MASKED, f32))
            highest = jnp.max(highest, axis=0, keepdims=True) * to_exp2

            def soft_step(ub, carry):
                total, att = carry
                keys = rows(ub, UB)
                p = jnp.exp2(scores[keys, :] * to_exp2 - highest)
                total = total + jnp.sum(p.reshape(UB // 8, 8, TB), axis=0)
                p = p.astype(bf16)
                probs[keys, :] = p
                return total, att + dot(v_t[head_rows, keys], p, ((1,), (0,)))

            total, att = lax.fori_loop(
                low, high, soft_step, (jnp.zeros((8, TB), f32), jnp.zeros((head_size, TB), f32))
            )
            inverse = 1.0 / jnp.sum(total, axis=0, keepdims=True)
            att = (att * inverse).astype(bf16).astype(f32)
            att_t[head_rows, here] = att
            do = do_t[head_rows, here].astype(bf16).astype(f32)
            delta = jnp.sum(do * att, axis=0, keepdims=True) * inverse
            do = (do * inverse).astype(bf16)
            parts = [do]
            if before:
                parts = [jnp.zeros((before, TB), bf16)] + parts
            if after:
                parts = parts + [jnp.zeros((after, TB), bf16)]
            do_wide = jnp.concatenate(parts, axis=0)

            def grad_step(ub, dq):
                keys = rows(ub, UB)
                p = probs[keys, :]
                dp = dot(qkv_ref[keys, pl.ds(2 * width + lane0, span)], do_wide, ((1,), (0,)))
                ds = (p.astype(f32) * (dp - delta)).astype(bf16)
                dk[keys, pl.ds(lane0, span)] += dot(ds, q, ((1,), (0,)))
                dv[keys, pl.ds(lane0, span)] += dot(p, do_wide, ((1,), (1,)))
                return dq + dot(k_t[head_rows, keys], ds, ((1,), (0,)))

            dq = lax.fori_loop(low, high, grad_step, jnp.zeros((head_size, TB), f32))
            dq_t[head_rows, here] = dq * scale
            return carry

        lax.fori_loop(0, time_rows // TB, time_block, 0)

    def results(c):
        here = rows(c, CH)
        lab = labb[here, :]
        for j in range(tiles):
            cols = pl.ds(j * LANES, LANES)
            out_ref[here, cols] = dq_t[cols, here].T.astype(bf16)
            out_ref[here, pl.ds(width + j * LANES, LANES)] = (dk[here, cols] * scale).astype(bf16)
            out_ref[here, pl.ds(2 * width + j * LANES, LANES)] = dv[here, cols].astype(bf16)
            val = att_t[cols, here].T
            for s in range(seg_count):
                there = pl.ds(pl.multiple_of(c * CH + GAP * s, GAP), CH)
                att_pad[there, cols] += jnp.where(lab == s + 1.0, val, 0.0)

    chunks(time_rows // CH, results)

    for j in range(tiles):
        cols = pl.ds(j * LANES, LANES)

        def tap_step(c, sums):
            r0 = c * 8
            att = att_pad[pl.ds(pl.multiple_of(r0, 8), 8), cols]
            return tuple(sums[w] + att * tap_view(w, r0, 8, cols) for w in range(taps))

        sums = lax.fori_loop(
            0, inner // 8, tap_step, tuple(jnp.zeros((8, LANES), f32) for _ in range(taps))
        )
        for w in range(taps):
            taps_ref[w : w + 1, cols] = jnp.sum(sums[w], axis=0, keepdims=True)
        taps_ref[taps : taps + 1, cols] = jnp.zeros((1, LANES), f32)


def run_block(bounds, qkv, cot, seg, cw, head_size):
    time_rows, width = cot.shape
    taps = cw.shape[0]
    f32, bf16 = jnp.float32, jnp.bfloat16
    inner = -(-(time_rows + GAP * 3) // 96) * 96
    rows_all = 23 * 48 + 8
    while rows_all < inner + 2 * GAP + 8:
        rows_all += 48
    vmem = pl.BlockSpec(memory_space=pltpu.VMEM)
    return pl.pallas_call(
        functools.partial(block_kernel, time_rows, width, head_size, taps),
        out_shape=(
            jax.ShapeDtypeStruct((time_rows, 3 * width), bf16),
            jax.ShapeDtypeStruct((taps + 1, width), f32),
        ),
        in_specs=[pl.BlockSpec(memory_space=pltpu.SMEM)] + [vmem] * 4,
        out_specs=(vmem, vmem),
        scratch_shapes=[
            pltpu.VMEM((time_rows, LANES), f32),
            pltpu.VMEM((time_rows, LANES), f32),
            pltpu.VMEM((8, rows_all, width), f32),
            pltpu.VMEM((inner, width), f32),
            pltpu.VMEM((rows_all, width), f32),
            pltpu.VMEM((width, time_rows), bf16),
            pltpu.VMEM((width, time_rows), bf16),
            pltpu.VMEM((width, time_rows), f32),
            pltpu.VMEM((width, time_rows), f32),
            pltpu.VMEM((width, time_rows), f32),
            pltpu.VMEM((time_rows, width), f32),
            pltpu.VMEM((time_rows, width), f32),
            pltpu.VMEM((time_rows, TB), f32),
            pltpu.VMEM((time_rows, TB), bf16),
        ],
        compiler_params=pltpu.CompilerParams(vmem_limit_bytes=56 * 1024 * 1024),
        cost_estimate=pl.CostEstimate(
            flops=14 * time_rows * time_rows * width, bytes_accessed=6 * time_rows * width * 2, transcendentals=0
        ),
    )(bounds, qkv, cot, seg, cw)


def local(qkv, grad_in, counts, segment, conv_weight):
    data_size = lax.axis_size("dp")
    time_size = lax.axis_size("seq")
    rows_here = qkv.shape[1]
    width = qkv.shape[2] // 3
    part = width // time_size
    head_size = width // H
    slot_rows = grad_in.shape[2]
    taps = conv_weight.shape[0]
    time_rows = rows_here * time_size

    filled = jnp.arange(slot_rows)[None, :] < counts[0][:, None]
    sent = jnp.where(filled[:, :, None], grad_in[0], jnp.asarray(EMPTY, jnp.bfloat16))
    sent = sent.reshape(data_size, slot_rows, time_size, part).transpose(0, 2, 1, 3)
    cot = lax.all_to_all(
        sent.reshape(data_size * time_size, slot_rows, part), ("dp", "seq"), 0, 0, tiled=True
    )
    cot = cot.reshape(data_size, time_size, slot_rows, part).transpose(1, 0, 2, 3)
    cot = cot.reshape(time_rows, part)

    mine = qkv[0].reshape(rows_here, 3, time_size, part).transpose(2, 0, 1, 3)
    mine = lax.all_to_all(mine.reshape(time_size, rows_here, 3 * part), "seq", 0, 0, tiled=True)
    mine = mine.reshape(time_rows, 3 * part)

    seg = lax.all_to_all(
        jnp.broadcast_to(segment[:, None, :], (time_size, 1, rows_here)), "seq", 0, 0, tiled=True
    ).reshape(time_rows)
    starts = seg[0::TB]
    ends = seg[TB - 1 :: TB]
    low = jnp.sum(seg[None, :] < starts[:, None], axis=1, dtype=jnp.int32)
    high = jnp.sum(seg[None, :] <= ends[:, None], axis=1, dtype=jnp.int32)
    bounds = jnp.stack([low // UB, (high + UB - 1) // UB], axis=1)
    weights = lax.dynamic_slice_in_dim(conv_weight, lax.axis_index("seq") * part, part, 1)

    grads, tap_terms = run_block(
        bounds, mine, cot, seg.astype(jnp.float32)[None, :], weights, head_size
    )

    grads = grads.reshape(time_size, data_size, slot_rows, 3 * part).transpose(1, 0, 2, 3)
    grads = lax.all_to_all(
        grads.reshape(data_size * time_size, slot_rows, 3 * part), ("dp", "seq"), 0, 0, tiled=True
    )
    grads = grads.reshape(data_size, time_size, slot_rows, 3, part).transpose(0, 2, 3, 1, 4)
    qkv_grad = grads.reshape(1, data_size, slot_rows, 3 * width)

    share = tap_terms.size // data_size
    terms = lax.all_to_all(tap_terms.reshape(data_size, 1, share), "dp", 0, 0, tiled=True)
    total = jnp.sum(terms, axis=0) / math.sqrt(data_size * slot_rows)
    total = lax.all_to_all(
        jnp.broadcast_to(total[None], (data_size, 1, share)), "dp", 0, 0, tiled=True
    ).reshape(taps + 1, part)
    total = lax.all_to_all(
        jnp.broadcast_to(total[None], (time_size, taps + 1, part)), "seq", 0, 0, tiled=True
    )
    conv_weight_grad = total.transpose(1, 0, 2).reshape(taps + 1, width)[:taps]
    return (qkv_grad, conv_weight_grad)


def solution(mesh):
    in_specs = (
        P("dp", "seq", None),
        P("dp", "seq", None, None),
        P("dp", "seq"),
        P("dp", "seq"),
        P(),
    )
    out_specs = (P("dp", "seq", None, None), P())
    return jax.shard_map(local, mesh=mesh, in_specs=in_specs, out_specs=out_specs, check_vma=False)
```

time: 811 us -> 290 us (0.36)
  waiting for transfers between devices: 358 us -> 103 us
  local copies, waits for them, and re-layouts: 177 us -> 36.8 us
  other arithmetic: 136 us -> 4.56 us
  Pallas kernels: 0 us -> 81.8 us
  matrix products: 59.3 us -> 0 us
  between operations: 14 us -> 0.79 us
    psum x1 -> x0, waiting for transfers between devices: 258 us -> none  [local(): tap_total = lax.psum(tap_terms, ('dp', 'seq'))]
    add x33 -> x0, other arithmetic: 106 us -> none  [the longest x31 106 us: tap_step(): grad_att + weight_row[None, :] * jnp.where(near[:, None], cot_in.astype(j...]
    all_to_all x2 -> x5, waiting for transfers between devices: 5.33 us -> 103 us  [the longest x1 58 us: local(): lax.all_to_all(grads.reshape(data_size * time_size, slot_rows, 3 * part),...]
    dynamic_slice x93 -> x1, local copies, waits for them, and re-layouts: 87.6 us -> 0.63 us  [local(): lax.dynamic_slice_in_dim(conv_weight, lax.axis_index('seq') * part, part, 1)]
    pallas_call x0 -> x1, Pallas kernels: none -> 81.8 us  [run_block(): pl.pallas_call(functools.partial(block_kernel, time_rows, width, head_siz...]
    reduce_scatter x1 -> x0, waiting for transfers between devices: 66.3 us -> none  [local(): lax.psum_scatter(key_terms.astype(jnp.bfloat16), 'seq', scatter_dimension...]
    dot_general x28 -> x0, matrix products: 59.3 us -> none  [the longest x4 14.1 us: gradients(): jnp.einsum('rhd,uhd->hru', dout_in, values_in, preferred_element_type=jnp...]
    dynamic_update_slice x31 -> x0, local copies, waits for them, and re-layouts: 44.7 us -> none  [tap_step(): grad_taps = lax.dynamic_update_index_in_dim(grad_taps, term, tap_index, 0)]
  transfers between devices with their start and end apart: 11 -> 5, of which waited for: 7 -> 3; matrix products, arithmetic and copies ran while one was open for 7% -> 7% of each run, Pallas kernels for 0% -> 0%
where the time goes in v1:
time: 290 us; the launch traced here: 289 us
  waiting for transfers between devices  103 us (36%)
  Pallas kernels  81.8 us (28%)
  local copies, waits for them, and re-layouts  36.8 us (13%)
  starting transfers between devices  34.1 us (12%)
  blocking collectives  28.6 us (10%)
  other arithmetic  4.56 us (2%)
    pallas_call x1, Pallas kernels, run_block(): pl.pallas_call(functools.partial(block_kernel, time_rows, width, head_siz...  81.8 us
    all_to_all x1, waiting for transfers between devices, local(): lax.all_to_all(grads.reshape(data_size * time_size, slot_rows, 3 * part),...  58 us
    all_to_all x1, waiting for transfers between devices, local(): lax.all_to_all(mine.reshape(time_size, rows_here, 3 * part), 'seq', 0, 0,...  23.6 us
    all_to_all x1, waiting for transfers between devices, local(): lax.all_to_all(sent.reshape(data_size * time_size, slot_rows, part), ('dp...  21.1 us
    all_to_all x1, starting transfers between devices, local(): lax.all_to_all(sent.reshape(data_size * time_size, slot_rows, part), ('dp...  15.4 us
    all_to_all x1, blocking collectives, local(): lax.all_to_all(tap_terms.reshape(data_size, 1, share), 'dp', 0, 0, tiled=...  14.9 us
    all_to_all x1, blocking collectives, local(): lax.all_to_all(jnp.broadcast_to(total[None], (data_size, 1, share)), 'dp'...  13.8 us
    unnamed x7, local copies, waits for them, and re-layouts  11.5 us
  transfers between devices with their start and end apart: 5, of which 3 were waited for; matrix products, arithmetic and copies ran while one was open for 7% of the time, Pallas kernels for 0%

profile of v1, /device:TPU:1, one launch (start us, length us, event | category | flops | bytes accessed | tf_op | source)
XLA Modules:
  0.0 289.3 jit_solution(9288676614353099894)
XLA Ops:
  0.6 0.0 copy-start
  0.6 1.3 broadcast_in_dim.23
  2.0 5.0 %all-to-all-start = ((s32[4,1,256]{2,1,0:T(1,128)}), s32[4,1,256]{2,1,0:T(1,128)S(1)}, u32[]{:S(2)}, u32[]{:S(2)}) async-start(s32[4,1,256]{2,1,0:T(1,128)} %broadcast_in_dim.23), calls=%async_computation | async-start | bytes 8192 | tf_op jit(solution)/shard_map/all_to_all | solution.py:312
  7.0 0.7 iota_compare_fusion
  7.7 1.6 bitcast_select_fusion
  9.3 0.3 fusion.4
  9.6 0.6 pad_maximum_fusion
  10.1 1.1 reshape.194
  11.2 0.0 all-to-all-done
  11.2 15.4 %all-to-all-start.2 = ((bf16[256,4,384]{2,1,0:T(4,128)(2,1)}), bf16[256,4,384]{2,1,0:T(4,128)(2,1)S(1)}, u32[]{:S(2)}, u32[]{:S(2)}) async-start(bf16[256,4,384]{2,1,0:T(4,128)(2,1)} %reshape.194), calls=%async_computation.2 | async-start | bytes 1572864 | tf_op jit(solution)/shard_map/all_to_all | solution.py:302
  26.7 2.8 copy.87
  29.5 1.6 copy.88
  31.1 21.1 %all-to-all-done.2 = bf16[256,4,384]{2,1,0:T(4,128)(2,1)S(1)} async-done(((bf16[256,4,384]{2,1,0:T(4,128)(2,1)}), bf16[256,4,384]{2,1,0:T(4,128)(2,1)S(1)}, u32[]{:S(2)}, u32[]{:S(2)}) %all-to-all-start.2) | async-done | bytes 786464 | tf_op jit(solution)/shard_map/all_to_all | solution.py:302
  52.1 3.6 %all-to-all-start.1 = ((bf16[4,256,1152]{1,2,0:T(8,128)(2,1)}), bf16[4,256,1152]{1,2,0:T(8,128)(2,1)S(1)}, u32[]{:S(2)}, u32[]{:S(2)}) async-start(bf16[4,256,1152]{1,2,0:T(8,128)(2,1)} %bitcast.6), calls=%async_computation.1 | async-start | bytes 4718592 | tf_op jit(solution)/shard_map/all_to_all | solution.py:309
  55.8 0.0 copy-done
  55.8 0.6 constant_dynamic-slice_fusion.cw_ref
  56.4 0.1 slice.24
  56.5 0.1 slice.25
  56.6 0.2 convert_reduce_fusion.1
  56.8 0.1 copy.83
  56.9 0.1 copy.79
  57.0 0.6 convert_element_type.21
  57.6 0.6 pad_add_fusion.bounds_ref
  58.2 1.2 copy.90
  59.4 2.3 reshape.196.cot_ref
  61.7 23.6 %all-to-all-done.1 = bf16[4,256,1152]{1,2,0:T(8,128)(2,1)S(1)} async-done(((bf16[4,256,1152]{1,2,0:T(8,128)(2,1)}), bf16[4,256,1152]{1,2,0:T(8,128)(2,1)S(1)}, u32[]{:S(2)}, u32[]{:S(2)}) %all-to-all-start.1) | async-done | bytes 2359328 | tf_op jit(solution)/shard_map/all_to_all | solution.py:309
  85.3 2.4 copy.89
  87.7 81.8 %shard_map.68 = (bf16[1024,1152]{1,0:T(8,128)(2,1)}, f32[32,384]{1,0:T(8,128)}) custom-call(s32[4,2]{1,0:T(4,128)} %pad_add_fusion.bounds_ref, bf16[1024,1152]{1,0:T(8,128)(2,1)} %bitcast.31, bf16[1024,384]{1,0:T(8,128)(2,1)} %reshape.196.cot_ref, f32[1,1024]{1,0:T(1,128)} %bitcast.38, f32[31,384]{1,0:T(8,128)} %constant_dynamic-slice_fusion.cw_ref), custom_call_target="tpu_custom_call" | custom-call | flops 5637144576 | bytes 4718592 | tf_op jit(solution)/shard_map/pallas_call | solution.py:257
  169.5 0.9 reshape.203
  170.4 14.9 %all_to_all.35 = f32[64,1,192]{2,1,0:T(1,128)S(1)} all-to-all(f32[64,1,192]{2,1,0:T(1,128)S(1)} %reshape.203), channel_id=1, replica_groups=mesh['dp'=64,'seq'=4] {'dp'}, dimensions={0} | all-to-all | bytes 98304 | tf_op jit(solution)/shard_map/all_to_all | solution.py:334
  185.3 0.1 reduce_sum.32
  185.4 13.8 %all_to_all.36 = f32[64,1,192]{2,1,0:T(1,128)S(1)} all-to-all(f32[64,1,192]{2,1,0:T(1,128)S(1)} %broadcast_in_dim.42), channel_id=1, replica_groups=mesh['dp'=64,'seq'=4] {'dp'}, dimensions={0} | all-to-all | bytes 98304 | tf_op jit(solution)/shard_map/all_to_all | solution.py:336
  199.2 0.2 reduce.1
  199.3 0.1 broadcast_in_dim.43
  199.4 0.7 broadcast_in_dim.44
  200.1 3.4 %all-to-all-start.6 = ((f32[4,32,384]{2,1,0:T(8,128)}), f32[4,32,384]{2,1,0:T(8,128)S(1)}, u32[]{:S(2)}, u32[]{:S(2)}) async-start(f32[4,32,384]{2,1,0:T(8,128)} %broadcast_in_dim.44), calls=%async_computation.6 | async-start | bytes 393216 | tf_op jit(solution)/shard_map/all_to_all | solution.py:339
  203.5 4.1 %reshape.197 = bf16[4,64,4,1152]{3,2,1,0:T(4,128)(2,1)S(1)} reshape(bf16[1024,1152]{1,0:T(8,128)(2,1)} %get-tuple-element.4) | data formatting | bytes 4718592 | tf_op jit(solution)/shard_map/reshape | solution.py:326
  207.6 2.2 copy.91
  209.8 0.0 all-to-all-done.6
  209.8 6.7 %all-to-all-start.3 = ((bf16[256,4,1152]{2,1,0:T(4,128)(2,1)}), bf16[256,4,1152]{2,1,0:T(4,128)(2,1)S(1)}, u32[]{:S(2)}, u32[]{:S(2)}) async-start(bf16[256,4,1152]{2,1,0:T(4,128)(2,1)} %bitcast.14), calls=%async_computation.3 | async-start | bytes 4718592 | tf_op jit(solution)/shard_map/all_to_all | solution.py:327
  216.5 0.1 copy.95
  216.6 0.7 copy.99
  217.3 58.0 %all-to-all-done.3 = bf16[256,4,1152]{2,1,0:T(4,128)(2,1)S(1)} async-done(((bf16[256,4,1152]{2,1,0:T(4,128)(2,1)}), bf16[256,4,1152]{2,1,0:T(4,128)(2,1)S(1)}, u32[]{:S(2)}, u32[]{:S(2)}) %all-to-all-start.3) | async-done | bytes 2359328 | tf_op jit(solution)/shard_map/all_to_all | solution.py:327
  275.3 1.7 copy.92
  277.0 4.4 %reshape.199 = bf16[64,4,4,3,384]{4,3,1,0,2:T(4,128)(2,1)S(1)} reshape(bf16[256,4,1152]{2,0,1:T(8,128)(2,1)} %copy.92) | data formatting | bytes 4718592 | tf_op jit(solution)/shard_map/reshape | solution.py:330
  281.4 2.6 copy.97
  284.0 5.3 %reshape.202 = bf16[1,64,4,4608]{3,2,1,0:T(4,128)(2,1)} reshape(bf16[64,4,3,4,384]{4,3,2,1,0:T(4,128)(2,1)} %copy.97) | data formatting | bytes 4718592
  (5 shorter events, 0.1 us)
Async XLA Ops:
  0.6 55.1 %copy-start = (f32[31,1536]{1,0:T(8,128)S(1)}, f32[31,1536]{1,0:T(8,128)}, u32[]{:S(2)}) copy-start(f32[31,1536]{1,0:T(8,128)} %param.9) | copy-start | bytes 571396
  2.0 9.2 %all-to-all-start = ((s32[4,1,256]{2,1,0:T(1,128)}), s32[4,1,256]{2,1,0:T(1,128)S(1)}, u32[]{:S(2)}, u32[]{:S(2)}) async-start(s32[4,1,256]{2,1,0:T(1,128)} %broadcast_in_dim.23), calls=%async_computation | async-start | bytes 8192 | tf_op jit(solution)/shard_map/all_to_all | solution.py:312
  11.2 40.9 %all-to-all-start.2 = ((bf16[256,4,384]{2,1,0:T(4,128)(2,1)}), bf16[256,4,384]{2,1,0:T(4,128)(2,1)S(1)}, u32[]{:S(2)}, u32[]{:S(2)}) async-start(bf16[256,4,384]{2,1,0:T(4,128)(2,1)} %reshape.194), calls=%async_computation.2 | async-start | bytes 1572864 | tf_op jit(solution)/shard_map/all_to_all | solution.py:302
  52.1 33.2 %all-to-all-start.1 = ((bf16[4,256,1152]{1,2,0:T(8,128)(2,1)}), bf16[4,256,1152]{1,2,0:T(8,128)(2,1)S(1)}, u32[]{:S(2)}, u32[]{:S(2)}) async-start(bf16[4,256,1152]{1,2,0:T(8,128)(2,1)} %bitcast.6), calls=%async_computation.1 | async-start | bytes 4718592 | tf_op jit(solution)/shard_map/all_to_all | solution.py:309
  200.1 9.7 %all-to-all-start.6 = ((f32[4,32,384]{2,1,0:T(8,128)}), f32[4,32,384]{2,1,0:T(8,128)S(1)}, u32[]{:S(2)}, u32[]{:S(2)}) async-start(f32[4,32,384]{2,1,0:T(8,128)} %broadcast_in_dim.44), calls=%async_computation.6 | async-start | bytes 393216 | tf_op jit(solution)/shard_map/all_to_all | solution.py:339
  209.8 65.5 %all-to-all-start.3 = ((bf16[256,4,1152]{2,1,0:T(4,128)(2,1)}), bf16[256,4,1152]{2,1,0:T(4,128)(2,1)S(1)}, u32[]{:S(2)}, u32[]{:S(2)}) async-start(bf16[256,4,1152]{2,1,0:T(4,128)(2,1)} %bitcast.14), calls=%async_computation.3 | async-start | bytes 4718592 | tf_op jit(solution)/shard_map/all_to_all | solution.py:327

commit v2 on v1

v2 whole, which is shorter than its diff:
```python
import functools
import math

import jax
import jax.numpy as jnp
from jax import lax
from jax.experimental import pallas as pl
from jax.experimental.pallas import tpu as pltpu
from jax.sharding import PartitionSpec as P

H = 16

EMPTY = 128.0
EMPTY_ABOVE = 64.0
MASKED = -1e30
LANES = 128
TB = 512
UB = 256
PAIR = 2
GAP = 16
SEGMENTS = 4
MESH = pl.DeviceIdType.MESH
CH = 128


def dot(a, b, contract):
    return lax.dot_general(a, b, (contract, ((), ())), preferred_element_type=jnp.float32)


def rows(index, size):
    return pl.ds(pl.multiple_of(index * size, size), size)


def chunks(count, body):
    def step(index, carry):
        body(index)
        return carry

    lax.fori_loop(0, count, step, 0)


def make_labels(time_rows, seg_ref, cot_ref, seg_row, labb):
    piece = seg_ref.shape[2]
    for s in range(seg_ref.shape[0]):
        seg_row[:, s * piece : (s + 1) * piece] = seg_ref[s].astype(jnp.float32)

    def step(c):
        here = rows(c, CH)
        across = jnp.broadcast_to(seg_row[:, here], (CH, CH)).T
        got = cot_ref[here, :LANES].astype(jnp.float32)
        labb[here, :] = jnp.where(got < EMPTY_ABOVE, across + 1.0, 0.0)

    chunks(time_rows // CH, step)


def make_shifted(time_rows, tiles, cot_ref, labb, shifted):
    rows_all = shifted.shape[1]

    def clear(c):
        shifted[0, rows(c, 8), :] = jnp.zeros((8, shifted.shape[2]), jnp.float32)

    chunks(rows_all // 8, clear)

    def spread(c):
        here = rows(c, CH)
        lab = labb[here, :]
        for j in range(tiles):
            cols = pl.ds(j * LANES, LANES)
            val = cot_ref[here, cols].astype(jnp.float32)
            for s in range(SEGMENTS):
                there = pl.ds(pl.multiple_of(c * CH + GAP * (s + 1), GAP), CH)
                shifted[0, there, cols] += jnp.where(lab == s + 1.0, val, 0.0)

    chunks(time_rows // CH, spread)

    def shift(c):
        r0 = pl.multiple_of(c * 48, 8)
        for j in range(tiles):
            cols = pl.ds(j * LANES, LANES)
            block = shifted[0, pl.ds(r0, 56), cols]
            for b in range(1, 8):
                shifted[b, pl.ds(r0, 48), cols] = block[b : b + 48]

    chunks((rows_all - 8) // 48, shift)


def tap_view(shifted, margin, w, r0, size, cols):
    offset = margin - w
    a, b = offset // 8, offset % 8
    return shifted[b, pl.ds(pl.multiple_of(r0 + GAP + 8 * a, 8), size), cols]


def block_kernel(
    time_rows,
    width,
    head_size,
    taps,
    qkv_ref,
    cot_ref,
    seg_ref,
    cw_ref,
    k_t,
    v_t,
    out_ref,
    att_ref,
    bounds,
    seg_row,
    labb,
    shifted,
    grad_pad,
    do_t,
    att_t,
    dq_t,
    dk,
    dv,
    scores,
    probs,
):
    f32, bf16 = jnp.float32, jnp.bfloat16
    margin = (taps - 1) // 2
    heads = width // head_size
    tiles = width // LANES
    scale = head_size ** (-0.5)

    make_labels(time_rows, seg_ref, cot_ref, seg_row, labb)
    make_shifted(time_rows, tiles, cot_ref, labb, shifted)

    def conv(c):
        r0 = c * 32
        for j in range(tiles):
            cols = pl.ds(j * LANES, LANES)
            total = jnp.zeros((32, LANES), f32)
            for w in range(taps):
                total = total + cw_ref[w : w + 1, cols] * tap_view(shifted, margin, w, r0, 32, cols)
            grad_pad[pl.ds(pl.multiple_of(r0, 16), 32), cols] = total

    chunks(grad_pad.shape[0] // 32, conv)

    def transposes(c):
        here = rows(c, CH)
        lab = labb[here, :]
        for j in range(tiles):
            cols = pl.ds(j * LANES, LANES)
            total = jnp.zeros((CH, LANES), f32)
            for s in range(SEGMENTS):
                there = pl.ds(pl.multiple_of(c * CH + GAP * s, GAP), CH)
                total = total + jnp.where(lab == s + 1.0, grad_pad[there, cols], 0.0)
            do_t[cols, here] = total.T
        dk[here, :] = jnp.zeros((CH, width), f32)
        dv[here, :] = jnp.zeros((CH, width), f32)

    chunks(time_rows // CH, transposes)

    everywhere = seg_row[...]
    for tb in range(time_rows // TB):
        mine = seg_row[:, tb * TB : (tb + 1) * TB]
        below = jnp.sum(jnp.where(everywhere < jnp.min(mine), 1, 0))
        upto = jnp.sum(jnp.where(everywhere <= jnp.max(mine), 1, 0))
        bounds[tb, 0] = below // UB
        bounds[tb, 1] = (upto + UB - 1) // UB

    cols_here = PAIR * TB
    row_index = lax.broadcasted_iota(jnp.int32, (UB, cols_here), 0)
    col_index = lax.broadcasted_iota(jnp.int32, (UB, cols_here), 1) % TB
    apart = col_index - row_index
    to_exp2 = scale * math.log2(math.e)

    for h0 in range(0, heads, PAIR):
        first, last = h0 * head_size, (h0 + PAIR) * head_size
        lane0 = first // LANES * LANES
        span = -(-last // LANES) * LANES - lane0
        lane = lax.broadcasted_iota(jnp.int32, (TB, span), 1) + lane0
        head_rows = [pl.ds((h0 + n) * head_size, head_size) for n in range(PAIR)]

        def beside(values):
            return jnp.concatenate(values, axis=1)

        def time_block(tb, carry):
            here = rows(tb, TB)
            low, high = bounds[tb, 0], bounds[tb, 1]
            q = qkv_ref[here, pl.ds(lane0, span)]
            q = jnp.concatenate(
                [
                    jnp.where(
                        (lane >= (h0 + n) * head_size) & (lane < (h0 + n + 1) * head_size),
                        q,
                        jnp.zeros((), bf16),
                    )
                    for n in range(PAIR)
                ],
                axis=0,
            )
            want = beside([seg_row[:, here] + 1.0] * PAIR)

            def score_step(ub, highest):
                keys = rows(ub, UB)
                s = dot(qkv_ref[keys, pl.ds(width + lane0, span)], q, ((1,), (1,)))
                lab = beside([labb[keys, :]] * (cols_here // LANES))
                ok = (lab == want) | (apart == ub * UB - tb * TB)
                s = jnp.where(ok, s, MASKED)
                scores[keys, :] = s
                return jnp.maximum(highest, jnp.max(s.reshape(UB // 8, 8, cols_here), axis=0))

            highest = lax.fori_loop(low, high, score_step, jnp.full((8, cols_here), MASKED, f32))
            highest = jnp.max(highest, axis=0, keepdims=True) * to_exp2
            for n in range(PAIR):
                att_t[head_rows[n], here] = jnp.zeros((head_size, TB), f32)
                dq_t[head_rows[n], here] = jnp.zeros((head_size, TB), f32)

            def soft_step(ub, total):
                keys = rows(ub, UB)
                p = jnp.exp2(scores[keys, :] * to_exp2 - highest)
                total = total + jnp.sum(p.reshape(UB // 8, 8, cols_here), axis=0)
                p = p.astype(bf16)
                probs[keys, :] = p
                for n in range(PAIR):
                    att_t[head_rows[n], here] += dot(
                        v_t[head_rows[n], keys], p[:, n * TB : (n + 1) * TB], ((1,), (0,))
                    )
                return total

            total = lax.fori_loop(low, high, soft_step, jnp.zeros((8, cols_here), f32))
            inverse = 1.0 / jnp.sum(total, axis=0, keepdims=True)
            deltas, wide = [], []
            for n in range(PAIR):
                inv = inverse[:, n * TB : (n + 1) * TB]
                att = (att_t[head_rows[n], here] * inv).astype(bf16).astype(f32)
                att_t[head_rows[n], here] = att
                do = do_t[head_rows[n], here].astype(bf16).astype(f32)
                deltas.append(jnp.sum(do * att, axis=0, keepdims=True) * inv)
                before = (h0 + n) * head_size - lane0
                after = span - before - head_size
                parts = [(do * inv).astype(bf16)]
                if before:
                    parts = [jnp.zeros((before, TB), bf16)] + parts
                if after:
                    parts = parts + [jnp.zeros((after, TB), bf16)]
                wide.append(jnp.concatenate(parts, axis=0))
            delta, do_wide = beside(deltas), beside(wide)

            def grad_step(ub, carry):
                keys = rows(ub, UB)
                p = probs[keys, :]
                dp = dot(qkv_ref[keys, pl.ds(2 * width + lane0, span)], do_wide, ((1,), (0,)))
                ds = (p.astype(f32) * (dp - delta)).astype(bf16)
                dk[keys, pl.ds(lane0, span)] += dot(ds, q, ((1,), (0,)))
                dv[keys, pl.ds(lane0, span)] += dot(p, do_wide, ((1,), (1,)))
                for n in range(PAIR):
                    dq_t[head_rows[n], here] += dot(
                        k_t[head_rows[n], keys], ds[:, n * TB : (n + 1) * TB], ((1,), (0,))
                    )
                return carry

            lax.fori_loop(low, high, grad_step, 0)
            return carry

        lax.fori_loop(0, time_rows // TB, time_block, 0)

    def results(c):
        here = rows(c, CH)
        lab = labb[here, :]
        for j in range(tiles):
            cols = pl.ds(j * LANES, LANES)
            out_ref[here, cols] = (dq_t[cols, here] * scale).T.astype(bf16)
            out_ref[here, pl.ds(width + j * LANES, LANES)] = (dk[here, cols] * scale).astype(bf16)
            out_ref[here, pl.ds(2 * width + j * LANES, LANES)] = dv[here, cols].astype(bf16)
            att_ref[here, cols] = att_t[cols, here].T.astype(bf16)

    chunks(time_rows // CH, results)
def flip_kernel(width, qkv_ref, k_t, v_t):
    def step(c):
        here = rows(c, CH)
        for j in range(width // LANES):
            cols = pl.ds(j * LANES, LANES)
            for n, target in ((1, k_t), (2, v_t)):
                target[cols, here] = qkv_ref[here, pl.ds(n * width + j * LANES, LANES)].T

    chunks(qkv_ref.shape[0] // CH, step)


def taps_kernel(time_rows, width, taps, seg_ref, cot_ref, att_ref, taps_ref, seg_row, labb, shifted, att_pad):
    f32 = jnp.float32
    tiles = width // LANES
    margin = (taps - 1) // 2
    inner = time_rows + GAP * (SEGMENTS - 1)
    make_labels(time_rows, seg_ref, cot_ref, seg_row, labb)
    make_shifted(time_rows, tiles, cot_ref, labb, shifted)

    def clear(c):
        att_pad[rows(c, 8), :] = jnp.zeros((8, width), f32)

    chunks(att_pad.shape[0] // 8, clear)

    def spread(c):
        here = rows(c, CH)
        lab = labb[here, :]
        for j in range(tiles):
            cols = pl.ds(j * LANES, LANES)
            val = att_ref[here, cols].astype(f32)
            for s in range(SEGMENTS):
                there = pl.ds(pl.multiple_of(c * CH + GAP * s, GAP), CH)
                att_pad[there, cols] += jnp.where(lab == s + 1.0, val, 0.0)

    chunks(time_rows // CH, spread)

    for j in range(tiles):
        cols = pl.ds(j * LANES, LANES)

        def tap_step(c, sums):
            r0 = c * 8
            att = att_pad[rows(c, 8), cols]
            return tuple(
                sums[w] + att * tap_view(shifted, margin, w, r0, 8, cols) for w in range(taps)
            )

        sums = lax.fori_loop(
            0, inner // 8, tap_step, tuple(jnp.zeros((8, LANES), f32) for _ in range(taps))
        )
        for w in range(taps):
            taps_ref[w : w + 1, cols] = jnp.sum(sums[w], axis=0, keepdims=True)
        taps_ref[taps : taps + 1, cols] = jnp.zeros((1, LANES), f32)


def padded_rows(time_rows):
    inner = -(-(time_rows + GAP * (SEGMENTS - 1)) // 96) * 96
    return inner, inner + 48 + 8


VMEM = pl.BlockSpec(memory_space=pltpu.VMEM)
ANY = pl.BlockSpec(memory_space=pl.ANY)
PARAMS = dict(vmem_limit_bytes=56 * 1024 * 1024)


def cost(flops, size):
    return pl.CostEstimate(flops=flops, bytes_accessed=size, transcendentals=0)


def flip(qkv, width):
    time_rows = qkv.shape[0]
    shape = jax.ShapeDtypeStruct((width, time_rows), jnp.bfloat16)
    return pl.pallas_call(
        functools.partial(flip_kernel, width),
        out_shape=(shape, shape),
        in_specs=[VMEM],
        out_specs=(VMEM, VMEM),
        compiler_params=pltpu.CompilerParams(**PARAMS),
        cost_estimate=cost(0, 16 * time_rows * width),
    )(qkv)


def run_taps(seg, cot, att, taps):
    time_rows, width = cot.shape
    f32 = jnp.float32
    inner, rows_all = padded_rows(time_rows)
    return pl.pallas_call(
        functools.partial(taps_kernel, time_rows, width, taps),
        out_shape=jax.ShapeDtypeStruct((taps + 1, width), f32),
        in_specs=[VMEM] * 3,
        out_specs=VMEM,
        scratch_shapes=[
            pltpu.VMEM((1, time_rows), f32),
            pltpu.VMEM((time_rows, LANES), f32),
            pltpu.VMEM((8, rows_all, width), f32),
            pltpu.VMEM((rows_all, width), f32),
        ],
        compiler_params=pltpu.CompilerParams(**PARAMS),
        cost_estimate=cost(1 << 33, 40 << 20),
    )(seg, cot, att)


def run_block(qkv, cot, seg, cw, k_t, v_t, head_size):
    time_rows, width = cot.shape
    taps = cw.shape[0]
    f32, bf16 = jnp.float32, jnp.bfloat16
    inner, rows_all = padded_rows(time_rows)
    return pl.pallas_call(
        functools.partial(block_kernel, time_rows, width, head_size, taps),
        out_shape=(
            jax.ShapeDtypeStruct((time_rows, 3 * width), bf16),
            jax.ShapeDtypeStruct((time_rows, width), bf16),
        ),
        in_specs=[VMEM] * 6,
        out_specs=(VMEM, VMEM),
        scratch_shapes=[
            pltpu.SMEM((time_rows // TB, 2), jnp.int32),
            pltpu.VMEM((1, time_rows), f32),
            pltpu.VMEM((time_rows, LANES), f32),
            pltpu.VMEM((8, rows_all, width), f32),
            pltpu.VMEM((inner, width), f32),
            pltpu.VMEM((width, time_rows), f32),
            pltpu.VMEM((width, time_rows), f32),
            pltpu.VMEM((width, time_rows), f32),
            pltpu.VMEM((time_rows, width), f32),
            pltpu.VMEM((time_rows, width), f32),
            pltpu.VMEM((time_rows, PAIR * TB), f32),
            pltpu.VMEM((time_rows, PAIR * TB), bf16),
        ],
        compiler_params=pltpu.CompilerParams(**PARAMS),
        cost_estimate=cost(14 * time_rows * time_rows * width, 12 * time_rows * width),
    )(qkv, cot, seg, cw, k_t, v_t)


def barrier(partners):
    sem = pltpu.get_barrier_semaphore()
    for partner in partners:
        pl.semaphore_signal(sem, inc=1, device_id=partner, device_id_type=MESH)
    pl.semaphore_wait(sem, len(partners))


def exchange_kernel(size, part, qkv_ref, seg_ref, out_ref, seg_out, send_sem, recv_sem, own_sem):
    me = lax.axis_index("seq")
    rows_here = qkv_ref.shape[0]
    width = part * size
    to = [lax.rem(me + k, size) for k in range(1, size)]
    barrier([{"seq": d} for d in to])

    def pieces(d):
        def cols(p):
            return pl.ds(pl.multiple_of(p * width + d * part, part), part)

        moves = [(seg_ref.at[0], seg_out.at[me])]
        for p in range(3):
            target = out_ref.at[rows(me, rows_here), pl.ds(p * part, part)]
            moves.append((qkv_ref.at[:, cols(p)], target))
        return moves

    copies = []
    for k in (2, 1, 3) if size == 4 else range(1, size):
        for n, (src, dst) in enumerate(pieces(to[k - 1])):
            copies.append(
                pltpu.make_async_remote_copy(
                    src_ref=src,
                    dst_ref=dst,
                    send_sem=send_sem.at[k - 1, n],
                    recv_sem=recv_sem.at[k - 1, n],
                    device_id={"seq": to[k - 1]},
                    device_id_type=MESH,
                )
            )
            copies[-1].start()
    own = []
    for n, (src, dst) in enumerate(pieces(me)):
        own.append(pltpu.make_async_copy(src, dst, own_sem.at[n]))
        own[-1].start()
    for copy in own + copies:
        copy.wait()


def exchange(qkv, seg, size):
    rows_here, columns = qkv.shape
    part = columns // 3 // size
    return pl.pallas_call(
        functools.partial(exchange_kernel, size, part),
        out_shape=(
            jax.ShapeDtypeStruct((rows_here * size, 3 * part), qkv.dtype),
            jax.ShapeDtypeStruct((size, 1, rows_here), seg.dtype),
        ),
        in_specs=[ANY, ANY],
        out_specs=(ANY, ANY),
        scratch_shapes=[
            pltpu.SemaphoreType.DMA((size - 1, 4)),
            pltpu.SemaphoreType.DMA((size - 1, 4)),
            pltpu.SemaphoreType.DMA((4,)),
        ],
        compiler_params=pltpu.CompilerParams(collective_id=1, has_side_effects=True),
        cost_estimate=cost(0, 64 << 20),
    )(qkv, seg[None])


def reduce_kernel(size, factor, terms_ref, out_ref, near, far, whole, send_sem, recv_sem):
    group = terms_ref.shape[0]
    data, me = lax.axis_index("dp"), lax.axis_index("seq")
    far_me, near_me = data // group, lax.rem(data, group)
    near_to = [lax.rem(near_me + k, group) for k in range(group)]
    far_to = [lax.rem(far_me + k, group) for k in range(group)]
    seq_to = [lax.rem(me + k, size) for k in range(size)]

    def device(z, n, s):
        return {"dp": z * group + n, "seq": s}

    last = [(k, m) for k in range(group) for m in range(size) if k or m]
    barrier(
        [device(far_me, near_to[k], seq_to[m]) for k, m in last]
        + [device(far_to[k], near_me, me) for k in range(1, group)]
    )
    used = [0]

    def send(src, dst, to):
        n = used[0]
        used[0] += 1
        copy = pltpu.make_async_remote_copy(
            src_ref=src,
            dst_ref=dst,
            send_sem=send_sem.at[n],
            recv_sem=recv_sem.at[n],
            device_id=to,
            device_id_type=MESH,
        )
        copy.start()
        return copy

    copies = [
        send(terms_ref.at[near_to[k]], near.at[k - 1], device(far_me, near_to[k], me))
        for k in range(1, group)
    ]
    for copy in copies:
        copy.wait()
    total = terms_ref[near_me]
    for k in range(1, group):
        total = total + near[k - 1]
    far[far_me] = total
    copies = [
        send(far.at[far_me], far.at[far_me], device(far_to[k], near_me, me)) for k in range(1, group)
    ]
    for copy in copies:
        copy.wait()
    total = far[0]
    for k in range(1, group):
        total = total + far[k]
    whole[me, near_me] = total * factor
    copies = [
        send(whole.at[me, near_me], whole.at[me, near_me], device(far_me, near_to[k], seq_to[m]))
        for k, m in last
    ]
    for copy in copies:
        copy.wait()
    out_ref[...] = whole[...]


def reduce_taps(terms, data_size, size, factor):
    taps, part = terms.shape
    group = math.isqrt(data_size)
    piece = (group, taps // group, part)
    sends = 2 * (group - 1) + group * size - 1
    whole = pl.pallas_call(
        functools.partial(reduce_kernel, size, factor),
        out_shape=jax.ShapeDtypeStruct((size,) + piece, terms.dtype),
        in_specs=[VMEM],
        out_specs=VMEM,
        scratch_shapes=[
            pltpu.VMEM(piece, terms.dtype),
            pltpu.VMEM(piece, terms.dtype),
            pltpu.VMEM((size,) + piece, terms.dtype),
            pltpu.SemaphoreType.DMA((sends,)),
            pltpu.SemaphoreType.DMA((sends,)),
        ],
        compiler_params=pltpu.CompilerParams(collective_id=2, has_side_effects=True),
        cost_estimate=cost(1 << 33, 40 << 20),
    )(terms.reshape(piece))
    return whole.reshape(size, taps, part).transpose(1, 0, 2).reshape(taps, size * part)


def gather_kernel(grads_ref, out_ref):
    size, _, _, columns = grads_ref.shape
    part = columns // 3
    for c in range(size):
        for p in range(3):
            out_ref[:, :, pl.ds((p * size + c) * part, part)] = grads_ref[c, :, :, pl.ds(p * part, part)]


def gather_parts(grads, size):
    blocks, slot_rows, columns = grads.shape
    count, step = blocks // size, 16
    return pl.pallas_call(
        gather_kernel,
        out_shape=jax.ShapeDtypeStruct((count, slot_rows, columns * size), grads.dtype),
        grid=(count // step,),
        in_specs=[pl.BlockSpec((size, step, slot_rows, columns), lambda g: (0, g, 0, 0))],
        out_specs=pl.BlockSpec((step, slot_rows, columns * size), lambda g: (g, 0, 0)),
        compiler_params=pltpu.CompilerParams(**PARAMS),
        cost_estimate=cost(0, 4 * blocks * slot_rows * columns),
    )(grads.reshape(size, count, slot_rows, columns))


def local(qkv, grad_in, counts, segment, conv_weight):
    data_size = lax.axis_size("dp")
    time_size = lax.axis_size("seq")
    rows_here = qkv.shape[1]
    width = qkv.shape[2] // 3
    part = width // time_size
    head_size = width // H
    slot_rows = grad_in.shape[2]
    taps = conv_weight.shape[0]
    time_rows = rows_here * time_size

    filled = jnp.arange(slot_rows)[None, :] < counts[0][:, None]
    sent = jnp.where(filled[:, :, None], grad_in[0], jnp.asarray(EMPTY, jnp.bfloat16))
    sent = sent.reshape(data_size, slot_rows, time_size, part).transpose(2, 0, 1, 3)
    cot = lax.all_to_all(
        sent.reshape(time_size * data_size, slot_rows, part), ("seq", "dp"), 0, 0, tiled=True
    )
    cot = cot.reshape(time_rows, part)

    mine, seg = exchange(qkv[0], segment, time_size)
    k_t, v_t = flip(mine, part)
    weights = lax.dynamic_slice_in_dim(conv_weight, lax.axis_index("seq") * part, part, 1)

    grads, att = run_block(mine, cot, seg, weights, k_t, v_t, head_size)
    grads = lax.all_to_all(
        grads.reshape(time_size * data_size, slot_rows, 3 * part), ("seq", "dp"), 0, 0, tiled=True
    )
    qkv_grad = gather_parts(grads, time_size)[None]

    tap_terms = run_taps(seg, cot, att, taps)
    factor = 1.0 / math.sqrt(data_size * slot_rows)
    conv_weight_grad = reduce_taps(tap_terms, data_size, time_size, factor)[:taps]
    return (qkv_grad, conv_weight_grad)


def solution(mesh):
    in_specs = (
        P("dp", "seq", None),
        P("dp", "seq", None, None),
        P("dp", "seq"),
        P("dp", "seq"),
        P(),
    )
    out_specs = (P("dp", "seq", None, None), P())
    return jax.shard_map(local, mesh=mesh, in_specs=in_specs, out_specs=out_specs, check_vma=False)
```

time: 290 us -> 191 us (0.66)
  waiting for transfers between devices: 103 us -> 0.01 us
  Pallas kernels: 81.8 us -> 140 us
  blocking collectives: 28.6 us -> 0 us
  local copies, waits for them, and re-layouts: 36.8 us -> 14.6 us
  other arithmetic: 4.56 us -> 1.39 us
    pallas_call x0 -> x5, Pallas kernels: none -> 112 us  [the longest x1 49.2 us: reduce_taps(): pl.pallas_call(functools.partial(reduce_kernel, size, factor), out_shape=...]
    all_to_all x5 -> x2, waiting for transfers between devices: 103 us -> 0.01 us  [the longest x1 0.01 us: local(): lax.all_to_all(grads.reshape(time_size * data_size, slot_rows, 3 * part),...]
    pallas_call x1, Pallas kernels: 81.8 us -> 28 us  [run_block(): pl.pallas_call(functools.partial(block_kernel, time_rows, width, head_siz...]
    all_to_all x2 -> x0, blocking collectives: 28.6 us -> none  [the longest x1 14.9 us: local(): lax.all_to_all(tap_terms.reshape(data_size, 1, share), 'dp', 0, 0, tiled=...]
    unnamed x7 -> x6, local copies, waits for them, and re-layouts: 11.5 us -> 2.15 us
    reshape x5 -> x3, local copies, waits for them, and re-layouts: 12.6 us -> 7.56 us  [the longest x1 5.13 us: local(): grads.reshape(time_size * data_size, slot_rows, 3 * part)]
    all_to_all x2 -> x0, local copies, waits for them, and re-layouts: 4.11 us -> none  [the longest x1 2.43 us: local(): lax.all_to_all(mine.reshape(time_size, rows_here, 3 * part), 'seq', 0, 0,...]
    all_to_all x5 -> x2, starting transfers between devices: 34.1 us -> 33.8 us  [the longest x1 18.2 us: local(): lax.all_to_all(grads.reshape(time_size * data_size, slot_rows, 3 * part),...]
  transfers between devices with their start and end apart: 5 -> 2, of which waited for: 3 -> 0; matrix products, arithmetic and copies ran while one was open for 7% -> 2% of each run, Pallas kernels for 0% -> 57%
where the time goes in v2:
time: 191 us; the launch traced here: 190 us
  Pallas kernels  140 us (73%)
  starting transfers between devices  33.8 us (18%)
  local copies, waits for them, and re-layouts  14.6 us (8%)
    pallas_call x1, Pallas kernels, reduce_taps(): pl.pallas_call(functools.partial(reduce_kernel, size, factor), out_shape=...  49.2 us
    pallas_call x1, Pallas kernels, exchange(): pl.pallas_call(functools.partial(exchange_kernel, size, part), out_shape=...  38.6 us
    pallas_call x1, Pallas kernels, run_block(): pl.pallas_call(functools.partial(block_kernel, time_rows, width, head_siz...  28 us
    all_to_all x1, starting transfers between devices, local(): lax.all_to_all(grads.reshape(time_size * data_size, slot_rows, 3 * part),...  18.2 us
    pallas_call x1, Pallas kernels, run_taps(): pl.pallas_call(functools.partial(taps_kernel, time_rows, width, taps), ou...  16.2 us
    all_to_all x1, starting transfers between devices, local(): lax.all_to_all(sent.reshape(time_size * data_size, slot_rows, part), ('se...  15.7 us
    reshape x1, local copies, waits for them, and re-layouts, local(): grads.reshape(time_size * data_size, slot_rows, 3 * part)  5.13 us
    pallas_call x1, Pallas kernels, gather_parts(): pl.pallas_call(gather_kernel, out_shape=jax.ShapeDtypeStruct((count, slot...  3.94 us
  transfers between devices with their start and end apart: 2, of which 0 were waited for; matrix products, arithmetic and copies ran while one was open for 2% of the time, Pallas kernels for 57%

profile of v2, /device:TPU:1, one launch (start us, length us, event | category | flops | bytes accessed | tf_op | source)
XLA Modules:
  0.0 190.2 jit_solution(9021240691139280997)
XLA Ops:
  0.6 0.0 copy-start
  0.6 0.8 iota_compare_fusion
  1.4 1.9 squeeze.7
  3.3 0.6 select_bitcast_fusion
  3.9 1.2 copy.7
  5.1 15.7 %all-to-all-start = ((bf16[256,4,384]{2,1,0:T(4,128)(2,1)}), bf16[256,4,384]{2,1,0:T(4,128)(2,1)S(1)}, u32[]{:S(2)}, u32[]{:S(2)}) async-start(bf16[256,4,384]{2,1,0:T(4,128)(2,1)} %bitcast.4), calls=%async_computation | async-start | bytes 1572864 | tf_op jit(solution)/shard_map/all_to_all | solution.py:589
  20.8 38.6 %shard_map.68 = (bf16[1024,1152]{1,0:T(8,128)(2,1)}, s32[4,1,256]{2,1,0:T(1,128)}) custom-call(bf16[256,4608]{1,0:T(8,128)(2,1)} %bitcast.14, s32[1,1,256]{2,1,0:T(1,128)} %bitcast.19), custom_call_target="tpu_custom_call" | custom-call | bytes 67108864 | tf_op jit(solution)/shard_map/pallas_call | solution.py:452
  59.4 3.7 %shard_map.69 = (bf16[384,1024]{1,0:T(8,128)(2,1)}, bf16[384,1024]{1,0:T(8,128)(2,1)}) custom-call(bf16[1024,1152]{1,0:T(8,128)(2,1)} %get-tuple-element.8.qkv_ref), custom_call_target="tpu_custom_call" | custom-call | bytes 6291456 | tf_op jit(solution)/shard_map/pallas_call | solution.py:341
  63.2 0.0 copy-done
  63.2 0.6 constant_dynamic-slice_fusion.cw_ref
  63.8 0.0 all-to-all-done
  63.8 1.1 reshape.51.cot_ref
  64.9 28.0 %shard_map.70 = (bf16[1024,1152]{1,0:T(8,128)(2,1)}, bf16[1024,384]{1,0:T(8,128)(2,1)}) custom-call(bf16[1024,1152]{1,0:T(8,128)(2,1)} %get-tuple-element.8.qkv_ref, bf16[1024,384]{1,0:T(8,128)(2,1)} %reshape.51.cot_ref, s32[4,1,256]{2,1,0:T(1,128)} %get-tuple-element.9.seg_ref, f32[31,384]{1,0:T(8,128)} %constant_dynamic-slice_fusion.cw_ref, ...), custom_call_target="tpu_custom_call" | custom-call | flops 5637144576 | bytes 4718592 | tf_op jit(solution)/shard_map/pallas_call | solution.py:376
  92.9 5.1 %reshape.52 = bf16[256,4,1152]{2,1,0:T(4,128)(2,1)} reshape(bf16[1024,1152]{1,0:T(8,128)(2,1)} %get-tuple-element.12) | data formatting | bytes 4718592 | tf_op jit(solution)/shard_map/reshape | solution.py:600
  98.0 18.2 %all-to-all-start.1 = ((bf16[256,4,1152]{2,1,0:T(4,128)(2,1)}), bf16[256,4,1152]{2,1,0:T(4,128)(2,1)S(1)}, u32[]{:S(2)}, u32[]{:S(2)}) async-start(bf16[256,4,1152]{2,1,0:T(4,128)(2,1)} %reshape.52), calls=%async_computation.1 | async-start | bytes 4718592 | tf_op jit(solution)/shard_map/all_to_all | solution.py:599
  116.2 16.2 %shard_map.72 = f32[32,384]{1,0:T(8,128)} custom-call(s32[4,1,256]{2,1,0:T(1,128)} %get-tuple-element.9.seg_ref, bf16[1024,384]{1,0:T(8,128)(2,1)} %reshape.51.cot_ref, bf16[1024,384]{1,0:T(8,128)(2,1)} %get-tuple-element.13.att_ref), custom_call_target="tpu_custom_call" | custom-call | flops 8589934592 | bytes 41943040 | tf_op jit(solution)/shard_map/pallas_call | solution.py:355
  132.4 1.4 reshape.54.terms_ref
  133.8 49.2 %shard_map.73 = f32[4,8,4,384]{3,2,1,0:T(4,128)} custom-call(f32[8,4,384]{2,1,0:T(4,128)} %reshape.54.terms_ref), custom_call_target="tpu_custom_call" | custom-call | flops 8589934592 | bytes 41943040 | tf_op jit(solution)/shard_map/pallas_call | solution.py:535
  183.0 1.0 reshape.55
  184.0 0.1 copy.8
  184.1 0.7 copy.9
  184.8 0.0 all-to-all-done.1
  184.8 0.0 copy-start.1
  184.8 1.4 copy-done.1
  186.3 3.9 %shard_map.71 = bf16[64,4,4608]{2,1,0:T(4,128)(2,1)} custom-call(bf16[4,64,4,1152]{3,2,1,0:T(4,128)(2,1)} %bitcast.13), custom_call_target="tpu_custom_call" | custom-call | bytes 4718592 | tf_op jit(solution)/shard_map/pallas_call | solution.py:564
  (1 shorter events, 0.0 us)
Async XLA Ops:
  0.6 62.5 %copy-start = (f32[31,1536]{1,0:T(8,128)S(1)}, f32[31,1536]{1,0:T(8,128)}, u32[]{:S(2)}) copy-start(f32[31,1536]{1,0:T(8,128)} %param.9) | copy-start | bytes 571396
  5.1 58.7 %all-to-all-start = ((bf16[256,4,384]{2,1,0:T(4,128)(2,1)}), bf16[256,4,384]{2,1,0:T(4,128)(2,1)S(1)}, u32[]{:S(2)}, u32[]{:S(2)}) async-start(bf16[256,4,384]{2,1,0:T(4,128)(2,1)} %bitcast.4), calls=%async_computation | async-start | bytes 1572864 | tf_op jit(solution)/shard_map/all_to_all | solution.py:589
  98.0 86.8 %all-to-all-start.1 = ((bf16[256,4,1152]{2,1,0:T(4,128)(2,1)}), bf16[256,4,1152]{2,1,0:T(4,128)(2,1)S(1)}, u32[]{:S(2)}, u32[]{:S(2)}) async-start(bf16[256,4,1152]{2,1,0:T(4,128)(2,1)} %reshape.52), calls=%async_computation.1 | async-start | bytes 4718592 | tf_op jit(solution)/shard_map/all_to_all | solution.py:599
  184.8 1.4 copy-start.1

commit v3 on v2

--- a/solution.py
+++ b/solution.py
@@ -407,64 +407,150 @@
     pl.semaphore_wait(sem, len(partners))
 
 
-def exchange_kernel(size, part, qkv_ref, seg_ref, out_ref, seg_out, send_sem, recv_sem, own_sem):
-    me = lax.axis_index("seq")
+def everyone(data_size, size, body):
+    group = math.isqrt(data_size)
+    data, me = lax.axis_index("dp"), lax.axis_index("seq")
+    far, near = data // group, lax.rem(data, group)
+    spread = [0]
+    for k in range(1, group // 2 + 1):
+        spread += [k, group - k] if 2 * k < group else [k]
+
+    def step(e, carry):
+        n = lax.rem(near + e, group)
+        for z in spread:
+            for m in range(size):
+                to = (lax.rem(far + z, group) * group + n, lax.rem(me + m, size))
+                if z or m:
+                    body(e, *to)
+                else:
+                    pl.when(e > 0)(functools.partial(body, e, *to))
+        return carry
+
+    lax.fori_loop(0, group, step, 0)
+
+
+def barrier_all(data_size, size):
+    sem = pltpu.get_barrier_semaphore()
+
+    def greet(e, dp, seq):
+        pl.semaphore_signal(sem, inc=1, device_id={"dp": dp, "seq": seq}, device_id_type=MESH)
+
+    everyone(data_size, size, greet)
+    pl.semaphore_wait(sem, data_size * size - 1)
+
+
+def arrive_kernel(
+    data_size, size, part, qkv_ref, sent_ref, seg_ref, out_ref, cot_ref, seg_out, send_sem, recv_sem, far_sem, own_sem
+):
+    data, me = lax.axis_index("dp"), lax.axis_index("seq")
+    group = math.isqrt(data_size)
     rows_here = qkv_ref.shape[0]
     width = part * size
-    to = [lax.rem(me + k, size) for k in range(1, size)]
-    barrier([{"seq": d} for d in to])
-
-    def pieces(d):
-        def cols(p):
-            return pl.ds(pl.multiple_of(p * width + d * part, part), part)
-
-        moves = [(seg_ref.at[0], seg_out.at[me])]
+    slice_rows = rows_here // group
+    to = [lax.rem(me + k, size) for k in range(size)]
+    barrier_all(data_size, size)
+
+    def cols(p, d):
+        return pl.ds(pl.multiple_of(p * width + d * part, part), part)
+
+    def near_copy(k, p, here, there):
+        return pltpu.make_async_remote_copy(
+            src_ref=qkv_ref.at[here, cols(p, to[k])],
+            dst_ref=out_ref.at[there, pl.ds(p * part, part)],
+            send_sem=send_sem.at[k - 1, p],
+            recv_sem=recv_sem.at[k - 1, p],
+            device_id={"seq": to[k]},
+            device_id_type=MESH,
+        )
+
+    def far_copy(dp, seq):
+        return pltpu.make_async_remote_copy(
+            src_ref=sent_ref.at[dp, :, pl.ds(pl.multiple_of(seq * part, part), part)],
+            dst_ref=cot_ref.at[me * data_size + data],
+            send_sem=far_sem.at[0],
+            recv_sem=far_sem.at[1],
+            device_id={"dp": dp, "seq": seq},
+            device_id_type=MESH,
+        )
+
+    def seg_copy(k):
+        return pltpu.make_async_remote_copy(
+            src_ref=seg_ref.at[0],
+            dst_ref=seg_out.at[me],
+            send_sem=send_sem.at[k - 1, 3],
+            recv_sem=recv_sem.at[k - 1, 3],
+            device_id={"seq": to[k]},
+            device_id_type=MESH,
+        )
+
+    for k in range(1, size):
+        seg_copy(k).start()
+    moves = [(seg_ref.at[0], seg_out.at[me])]
+    moves.append((sent_ref.at[data, :, cols(0, me)], cot_ref.at[me * data_size + data]))
+    for p in range(3):
+        moves.append((qkv_ref.at[:, cols(p, me)], out_ref.at[rows(me, rows_here), pl.ds(p * part, part)]))
+    own = [pltpu.make_async_copy(src, dst, own_sem.at[n]) for n, (src, dst) in enumerate(moves)]
+    for copy in own:
+        copy.start()
+
+    far, near = data // group, lax.rem(data, group)
+    spread = [0, 4, 1, 7, 2, 6, 3, 5] if group == 8 else list(range(group))
+
+    def step(e, carry):
+        n = lax.rem(near + e, group)
+        here = rows(e, slice_rows)
+        there = pl.ds(pl.multiple_of(me * rows_here + e * slice_rows, slice_rows), slice_rows)
+        near_left = [(k, p) for p in range(3) for k in range(1, size)]
+        for z in spread:
+            for k, p in near_left[:2]:
+                near_copy(k, p, here, there).start()
+            near_left = near_left[2:]
+            for m in range(size):
+                dp, seq = lax.rem(far + z, group) * group + n, to[m]
+                if z or m:
+                    far_copy(dp, seq).start()
+                else:
+
+                    @pl.when(e > 0)
+                    def _():
+                        far_copy(dp, seq).start()
+
+        return carry
+
+    lax.fori_loop(0, group, step, 0)
+    for copy in own:
+        copy.wait()
+    for k in range(1, size):
+        seg_copy(k).wait()
         for p in range(3):
-            target = out_ref.at[rows(me, rows_here), pl.ds(p * part, part)]
-            moves.append((qkv_ref.at[:, cols(p)], target))
-        return moves
-
-    copies = []
-    for k in (2, 1, 3) if size == 4 else range(1, size):
-        for n, (src, dst) in enumerate(pieces(to[k - 1])):
-            copies.append(
-                pltpu.make_async_remote_copy(
-                    src_ref=src,
-                    dst_ref=dst,
-                    send_sem=send_sem.at[k - 1, n],
-                    recv_sem=recv_sem.at[k - 1, n],
-                    device_id={"seq": to[k - 1]},
-                    device_id_type=MESH,
-                )
-            )
-            copies[-1].start()
-    own = []
-    for n, (src, dst) in enumerate(pieces(me)):
-        own.append(pltpu.make_async_copy(src, dst, own_sem.at[n]))
-        own[-1].start()
-    for copy in own + copies:
-        copy.wait()
-
-
-def exchange(qkv, seg, size):
+            near_copy(k, p, pl.ds(0, rows_here), rows(me, rows_here)).wait()
+    others = cot_ref.at[pl.ds(0, data_size * size - 1)]
+    pltpu.make_async_copy(others, others, far_sem.at[0]).wait()
+    pltpu.make_async_copy(others, others, far_sem.at[1]).wait()
+
+
+def arrive(qkv, sent, seg, data_size, size):
     rows_here, columns = qkv.shape
     part = columns // 3 // size
+    slot_rows = sent.shape[1]
     return pl.pallas_call(
-        functools.partial(exchange_kernel, size, part),
+        functools.partial(arrive_kernel, data_size, size, part),
         out_shape=(
             jax.ShapeDtypeStruct((rows_here * size, 3 * part), qkv.dtype),
+            jax.ShapeDtypeStruct((size * data_size, slot_rows, part), sent.dtype),
             jax.ShapeDtypeStruct((size, 1, rows_here), seg.dtype),
         ),
-        in_specs=[ANY, ANY],
-        out_specs=(ANY, ANY),
+        in_specs=[ANY, ANY, ANY],
+        out_specs=(ANY, ANY, ANY),
         scratch_shapes=[
             pltpu.SemaphoreType.DMA((size - 1, 4)),
             pltpu.SemaphoreType.DMA((size - 1, 4)),
-            pltpu.SemaphoreType.DMA((4,)),
+            pltpu.SemaphoreType.DMA((2,)),
+            pltpu.SemaphoreType.DMA((5,)),
         ],
         compiler_params=pltpu.CompilerParams(collective_id=1, has_side_effects=True),
         cost_estimate=cost(0, 64 << 20),
-    )(qkv, seg[None])
+    )(qkv, sent, seg[None])
 
 
 def reduce_kernel(size, factor, terms_ref, out_ref, near, far, whole, send_sem, recv_sem):
@@ -585,13 +671,8 @@
 
     filled = jnp.arange(slot_rows)[None, :] < counts[0][:, None]
     sent = jnp.where(filled[:, :, None], grad_in[0], jnp.asarray(EMPTY, jnp.bfloat16))
-    sent = sent.reshape(data_size, slot_rows, time_size, part).transpose(2, 0, 1, 3)
-    cot = lax.all_to_all(
-        sent.reshape(time_size * data_size, slot_rows, part), ("seq", "dp"), 0, 0, tiled=True
-    )
+    mine, cot, seg = arrive(qkv[0], sent, segment, data_size, time_size)
     cot = cot.reshape(time_rows, part)
-
-    mine, seg = exchange(qkv[0], segment, time_size)
     k_t, v_t = flip(mine, part)
     weights = lax.dynamic_slice_in_dim(conv_weight, lax.axis_index("seq") * part, part, 1)
 

time: 191 us -> 184 us (0.963)
  starting transfers between devices: 33.8 us -> 14.5 us
  Pallas kernels: 140 us -> 152 us
    all_to_all x1 -> x0, starting transfers between devices: 15.7 us -> none  [local(): lax.all_to_all(sent.reshape(time_size * data_size, slot_rows, part), ('se...]
    pallas_call x1, Pallas kernels: 38.6 us -> 51.3 us  [arrive(): pl.pallas_call(functools.partial(arrive_kernel, data_size, size, part), o...]
    all_to_all x1, starting transfers between devices: 18.2 us -> 14.5 us  [local(): lax.all_to_all(grads.reshape(time_size * data_size, slot_rows, 3 * part),...]
    select_n x0 -> x1, other arithmetic: none -> 2.44 us  [local(): jnp.where(filled[:, :, None], grad_in[0], jnp.asarray(EMPTY, jnp.bfloat16))]
  transfers between devices with their start and end apart: 2 -> 1, of which waited for: 0 -> 0; matrix products, arithmetic and copies ran while one was open for 2% -> 2% of each run, Pallas kernels for 57% -> 36%
where the time goes in v3:
time: 184 us; the launch traced here: 183 us
  Pallas kernels  152 us (83%)
  starting transfers between devices  14.5 us (8%)
  local copies, waits for them, and re-layouts  12.7 us (7%)
  other arithmetic  3.21 us (2%)
    pallas_call x1, Pallas kernels, arrive(): pl.pallas_call(functools.partial(arrive_kernel, data_size, size, part), o...  51.3 us
    pallas_call x1, Pallas kernels, reduce_taps(): pl.pallas_call(functools.partial(reduce_kernel, size, factor), out_shape=...  49.2 us
    pallas_call x1, Pallas kernels, run_block(): pl.pallas_call(functools.partial(block_kernel, time_rows, width, head_siz...  28 us
    pallas_call x1, Pallas kernels, run_taps(): pl.pallas_call(functools.partial(taps_kernel, time_rows, width, taps), ou...  16.2 us
    all_to_all x1, starting transfers between devices, local(): lax.all_to_all(grads.reshape(time_size * data_size, slot_rows, 3 * part),...  14.5 us
    reshape x1, local copies, waits for them, and re-layouts, local(): grads.reshape(time_size * data_size, slot_rows, 3 * part)  5.12 us
    pallas_call x1, Pallas kernels, gather_parts(): pl.pallas_call(gather_kernel, out_shape=jax.ShapeDtypeStruct((count, slot...  3.94 us
    pallas_call x1, Pallas kernels, flip(): pl.pallas_call(functools.partial(flip_kernel, width), out_shape=(shape, s...  3.72 us
  transfers between devices with their start and end apart: 1, of which 0 were waited for; matrix products, arithmetic and copies ran while one was open for 2% of the time, Pallas kernels for 36%

profile of v3, /device:TPU:1, one launch (start us, length us, event | category | flops | bytes accessed | tf_op | source)
XLA Modules:
  0.0 183.4 jit_solution(18329537583646372282)
XLA Ops:
  0.6 0.0 copy-start
  0.6 0.8 iota_compare_fusion
  1.4 2.4 %bitcast_select_fusion.sent_ref = bf16[64,4,1536]{2,1,0:T(4,128)(2,1)} fusion(bf16[1,64,4,1536]{3,2,1,0:T(4,128)(2,1)} %param.6, pred[64,4]{1,0:T(8,128)(4,1)S(1)} %iota_compare_fusion), kind=kLoop, calls=%fused_computation | loop fusion | flops 393216 | bytes 1573120 | tf_op jit(solution)/shard_map/jit(_where)/select_n | solution.py:673
  3.9 51.3 %shard_map.68 = (bf16[1024,1152]{1,0:T(8,128)(2,1)}, bf16[256,4,384]{2,1,0:T(4,128)(2,1)}, s32[4,1,256]{2,1,0:T(1,128)}) custom-call(bf16[256,4608]{1,0:T(8,128)(2,1)} %bitcast.13, bf16[64,4,1536]{2,1,0:T(4,128)(2,1)} %bitcast_select_fusion.sent_ref, s32[1,1,256]{2,1,0:T(1,128)} %bitcast.18), custom_call_target="tpu_custom_call" | custom-call | bytes 67108864 | tf_op jit(solution)/shard_map/pallas_call | solution.py:536
  55.2 2.3 %reshape.45.cot_ref = bf16[1024,384]{1,0:T(8,128)(2,1)} reshape(bf16[256,4,384]{2,1,0:T(4,128)(2,1)} %get-tuple-element.10) | data formatting | bytes 1572864 | tf_op jit(solution)/shard_map/reshape | solution.py:675
  57.5 3.7 %shard_map.69 = (bf16[384,1024]{1,0:T(8,128)(2,1)}, bf16[384,1024]{1,0:T(8,128)(2,1)}) custom-call(bf16[1024,1152]{1,0:T(8,128)(2,1)} %get-tuple-element.9.qkv_ref), custom_call_target="tpu_custom_call" | custom-call | bytes 6291456 | tf_op jit(solution)/shard_map/pallas_call | solution.py:341
  61.2 0.0 copy-done
  61.2 0.6 constant_dynamic-slice_fusion.cw_ref
  61.8 28.0 %shard_map.70 = (bf16[1024,1152]{1,0:T(8,128)(2,1)}, bf16[1024,384]{1,0:T(8,128)(2,1)}) custom-call(bf16[1024,1152]{1,0:T(8,128)(2,1)} %get-tuple-element.9.qkv_ref, bf16[1024,384]{1,0:T(8,128)(2,1)} %reshape.45.cot_ref, s32[4,1,256]{2,1,0:T(1,128)} %get-tuple-element.11.seg_ref, f32[31,384]{1,0:T(8,128)} %constant_dynamic-slice_fusion.cw_ref, ...), custom_call_target="tpu_custom_call" | custom-call | flops 5637144576 | bytes 4718592 | tf_op jit(solution)/shard_map/pallas_call | solution.py:376
  89.8 5.1 %reshape.46 = bf16[256,4,1152]{2,1,0:T(4,128)(2,1)} reshape(bf16[1024,1152]{1,0:T(8,128)(2,1)} %get-tuple-element.14) | data formatting | bytes 4718592 | tf_op jit(solution)/shard_map/reshape | solution.py:681
  95.0 14.5 %all-to-all-start = ((bf16[256,4,1152]{2,1,0:T(4,128)(2,1)}), bf16[256,4,1152]{2,1,0:T(4,128)(2,1)S(1)}, u32[]{:S(2)}, u32[]{:S(2)}) async-start(bf16[256,4,1152]{2,1,0:T(4,128)(2,1)} %reshape.46), calls=%async_computation | async-start | bytes 4718592 | tf_op jit(solution)/shard_map/all_to_all | solution.py:680
  109.4 16.2 %shard_map.72 = f32[32,384]{1,0:T(8,128)} custom-call(s32[4,1,256]{2,1,0:T(1,128)} %get-tuple-element.11.seg_ref, bf16[1024,384]{1,0:T(8,128)(2,1)} %reshape.45.cot_ref, bf16[1024,384]{1,0:T(8,128)(2,1)} %get-tuple-element.15.att_ref), custom_call_target="tpu_custom_call" | custom-call | flops 8589934592 | bytes 41943040 | tf_op jit(solution)/shard_map/pallas_call | solution.py:355
  125.6 1.4 reshape.48.terms_ref
  127.0 49.2 %shard_map.73 = f32[4,8,4,384]{3,2,1,0:T(4,128)} custom-call(f32[8,4,384]{2,1,0:T(4,128)} %reshape.48.terms_ref), custom_call_target="tpu_custom_call" | custom-call | flops 8589934592 | bytes 41943040 | tf_op jit(solution)/shard_map/pallas_call | solution.py:621
  176.2 1.0 reshape.49
  177.2 0.1 copy.7
  177.4 0.7 copy.8
  178.1 0.0 all-to-all-done
  178.1 0.0 copy-start.1
  178.1 1.4 copy-done.1
  179.5 3.9 %shard_map.71 = bf16[64,4,4608]{2,1,0:T(4,128)(2,1)} custom-call(bf16[4,64,4,1152]{3,2,1,0:T(4,128)(2,1)} %bitcast.12), custom_call_target="tpu_custom_call" | custom-call | bytes 4718592 | tf_op jit(solution)/shard_map/pallas_call | solution.py:650
  (1 shorter events, 0.0 us)
Async XLA Ops:
  0.6 60.6 %copy-start = (f32[31,1536]{1,0:T(8,128)S(1)}, f32[31,1536]{1,0:T(8,128)}, u32[]{:S(2)}) copy-start(f32[31,1536]{1,0:T(8,128)} %param.9) | copy-start | bytes 571396
  95.0 83.1 %all-to-all-start = ((bf16[256,4,1152]{2,1,0:T(4,128)(2,1)}), bf16[256,4,1152]{2,1,0:T(4,128)(2,1)S(1)}, u32[]{:S(2)}, u32[]{:S(2)}) async-start(bf16[256,4,1152]{2,1,0:T(4,128)(2,1)} %reshape.46), calls=%async_computation | async-start | bytes 4718592 | tf_op jit(solution)/shard_map/all_to_all | solution.py:680
  178.1 1.4 copy-start.1

commit v4 on v1

v4 whole, which is shorter than its diff:
```python
import functools
import math

import jax
import jax.numpy as jnp
from jax import lax
from jax.experimental import pallas as pl
from jax.experimental.pallas import tpu as pltpu
from jax.sharding import PartitionSpec as P

H = 16

EMPTY = 128.0
EMPTY_ABOVE = 64.0
MASKED = -1e30
LANES = 128
TB = 512
UB = 256
SLICE = 16
PAIR = 2
GAP = 16
SEGMENTS = 4
MESH = pl.DeviceIdType.MESH
CH = 128


def dot(a, b, contract):
    return lax.dot_general(a, b, (contract, ((), ())), preferred_element_type=jnp.float32)


def rows(index, size):
    return pl.ds(pl.multiple_of(index * size, size), size)


def chunks(count, body):
    def step(index, carry):
        body(index)
        return carry

    lax.fori_loop(0, count, step, 0)


def tap_view(shifted, margin, w, r0, size, cols):
    offset = margin - w
    a, b = offset // 8, offset % 8
    return shifted[b, pl.ds(pl.multiple_of(r0 + GAP + 8 * a, 8), size), cols]


def clear(ref):
    def step(c):
        ref[rows(c, 8), :] = jnp.zeros((8, ref.shape[1]), ref.dtype)

    chunks(ref.shape[0] // 8, step)


def spread_rows(value, labb, target, time_rows, shift, tiles):
    def step(c):
        lab = labb[rows(c, CH), :]
        for j in range(tiles):
            val = value(c, j)
            for s in range(SEGMENTS):
                there = pl.ds(pl.multiple_of(c * CH + GAP * (s + shift), GAP), CH)
                target[there, pl.ds(j * LANES, LANES)] += jnp.where(lab == s + 1.0, val, 0.0)

    chunks(time_rows // CH, step)


def convolve(time_rows, tiles, taps, cols_of, cot, seg_ref, cw_ref, seg_row, labb, shifted, grad_pad, do_t):
    f32 = jnp.float32
    margin = (taps - 1) // 2
    slots = cot.shape[1]
    piece = seg_ref.shape[2]
    for s in range(seg_ref.shape[0]):
        seg_row[:, s * piece : (s + 1) * piece] = seg_ref[s].astype(f32)

    def cot_rows(c, j):
        val = cot[rows(c, CH // slots), :, pl.ds(j * LANES, LANES)].astype(f32)
        return val.reshape(CH, LANES)

    def label(c):
        here = rows(c, CH)
        across = jnp.broadcast_to(seg_row[:, here], (CH, CH)).T
        labb[here, :] = jnp.where(cot_rows(c, 0) < EMPTY_ABOVE, across + 1.0, 0.0)

    chunks(time_rows // CH, label)
    spread_rows(cot_rows, labb, shifted.at[0], time_rows, 1, tiles)

    def shift(c):
        r0 = pl.multiple_of(c * 48, 8)
        for j in range(tiles):
            cols = pl.ds(j * LANES, LANES)
            block = shifted[0, pl.ds(r0, 56), cols]
            for b in range(1, 8):
                shifted[b, pl.ds(r0, 48), cols] = block[b : b + 48]

    chunks((shifted.shape[1] - 8) // 48, shift)

    def conv(c):
        r0 = c * 32
        for j in range(tiles):
            cols = pl.ds(j * LANES, LANES)
            total = jnp.zeros((32, LANES), f32)
            for w in range(taps):
                weight = cw_ref[w : w + 1, cols_of(j)]
                total = total + weight * tap_view(shifted, margin, w, r0, 32, cols)
            grad_pad[pl.ds(pl.multiple_of(r0, 16), 32), cols] = total

    chunks(grad_pad.shape[0] // 32, conv)

    def collect(c):
        lab = labb[rows(c, CH), :]
        for j in range(tiles):
            cols = pl.ds(j * LANES, LANES)
            total = jnp.zeros((CH, LANES), f32)
            for s in range(SEGMENTS):
                there = pl.ds(pl.multiple_of(c * CH + GAP * s, GAP), CH)
                total = total + jnp.where(lab == s + 1.0, grad_pad[there, cols], 0.0)
            do_t[cols, rows(c, CH)] = total.T

    chunks(time_rows // CH, collect)


def attend(time_rows, width, head_size, qkv_ref, seg_row, labb, k_t, v_t, do_t, att_t, dq_t, dk, dv, scores, probs):
    f32, bf16 = jnp.float32, jnp.bfloat16
    heads = width // head_size
    scale = head_size ** (-0.5)

    def flip(c):
        here = rows(c, CH)
        for j in range(width // LANES):
            cols = pl.ds(j * LANES, LANES)
            for n, target in ((1, k_t), (2, v_t)):
                target[cols, here] = qkv_ref[here, pl.ds(n * width + j * LANES, LANES)].T

    chunks(time_rows // CH, flip)
    cols_here = PAIR * TB
    row_index = lax.broadcasted_iota(jnp.int32, (UB, cols_here), 0)
    col_index = lax.broadcasted_iota(jnp.int32, (UB, cols_here), 1) % TB
    apart = col_index - row_index
    to_exp2 = scale * math.log2(math.e)

    for h0 in range(0, heads, PAIR):
        first, last = h0 * head_size, (h0 + PAIR) * head_size
        lane0 = first // LANES * LANES
        span = -(-last // LANES) * LANES - lane0
        lane = lax.broadcasted_iota(jnp.int32, (TB, span), 1) + lane0
        head_rows = [pl.ds((h0 + n) * head_size, head_size) for n in range(PAIR)]

        def beside(values):
            return jnp.concatenate(values, axis=1)

        def time_block(tb, carry):
            here = rows(tb, TB)
            low, high = 0, time_rows // UB
            q = qkv_ref[here, pl.ds(lane0, span)]
            q = jnp.concatenate(
                [
                    jnp.where(
                        (lane >= (h0 + n) * head_size) & (lane < (h0 + n + 1) * head_size),
                        q,
                        jnp.zeros((), bf16),
                    )
                    for n in range(PAIR)
                ],
                axis=0,
            )
            want = beside([seg_row[:, here] + 1.0] * PAIR)

            def score_step(ub, highest):
                keys = rows(ub, UB)
                s = dot(qkv_ref[keys, pl.ds(width + lane0, span)], q, ((1,), (1,)))
                lab = beside([labb[keys, :]] * (cols_here // LANES))
                ok = (lab == want) | (apart == ub * UB - tb * TB)
                s = jnp.where(ok, s, MASKED)
                scores[keys, :] = s
                return jnp.maximum(highest, jnp.max(s.reshape(UB // 8, 8, cols_here), axis=0))

            highest = lax.fori_loop(low, high, score_step, jnp.full((8, cols_here), MASKED, f32))
            highest = jnp.max(highest, axis=0, keepdims=True) * to_exp2
            for n in range(PAIR):
                att_t[head_rows[n], here] = jnp.zeros((head_size, TB), f32)
                dq_t[head_rows[n], here] = jnp.zeros((head_size, TB), f32)

            def soft_step(ub, total):
                keys = rows(ub, UB)
                p = jnp.exp2(scores[keys, :] * to_exp2 - highest)
                total = total + jnp.sum(p.reshape(UB // 8, 8, cols_here), axis=0)
                p = p.astype(bf16)
                probs[keys, :] = p
                for n in range(PAIR):
                    att_t[head_rows[n], here] += dot(
                        v_t[head_rows[n], keys], p[:, n * TB : (n + 1) * TB], ((1,), (0,))
                    )
                return total

            total = lax.fori_loop(low, high, soft_step, jnp.zeros((8, cols_here), f32))
            inverse = 1.0 / jnp.sum(total, axis=0, keepdims=True)
            deltas, wide = [], []
            for n in range(PAIR):
                inv = inverse[:, n * TB : (n + 1) * TB]
                att = (att_t[head_rows[n], here] * inv).astype(bf16).astype(f32)
                att_t[head_rows[n], here] = att
                do = do_t[head_rows[n], here].astype(bf16).astype(f32)
                deltas.append(jnp.sum(do * att, axis=0, keepdims=True) * inv)
                before = (h0 + n) * head_size - lane0
                after = span - before - head_size
                parts = [(do * inv).astype(bf16)]
                if before:
                    parts = [jnp.zeros((before, TB), bf16)] + parts
                if after:
                    parts = parts + [jnp.zeros((after, TB), bf16)]
                wide.append(jnp.concatenate(parts, axis=0))
            delta, do_wide = beside(deltas), beside(wide)

            def grad_step(ub, carry):
                keys = rows(ub, UB)
                p = probs[keys, :]
                dp = dot(qkv_ref[keys, pl.ds(2 * width + lane0, span)], do_wide, ((1,), (0,)))
                ds = (p.astype(f32) * (dp - delta)).astype(bf16)
                dk[keys, pl.ds(lane0, span)] += dot(ds, q, ((1,), (0,)))
                dv[keys, pl.ds(lane0, span)] += dot(p, do_wide, ((1,), (1,)))
                for n in range(PAIR):
                    dq_t[head_rows[n], here] += dot(
                        k_t[head_rows[n], keys], ds[:, n * TB : (n + 1) * TB], ((1,), (0,))
                    )
                return carry

            lax.fori_loop(low, high, grad_step, 0)
            return carry

        lax.fori_loop(0, time_rows // TB, time_block, 0)


def block_kernel(
    data_size,
    size,
    head_size,
    factor,
    qkv_ref,
    sent_ref,
    seg_ref,
    cw_ref,
    out_ref,
    taps_ref,
    seg_all,
    mine,
    cot,
    stage,
    seg_row,
    labb,
    shifted,
    grad_pad,
    att_pad,
    k_t,
    v_t,
    do_t,
    att_t,
    dq_t,
    dk,
    dv,
    scores,
    probs,
    terms,
    near_sum,
    far_sum,
    whole,
    own_sem,
    seq_send,
    seq_recv,
    in_send,
    in_recv,
    out_send,
    out_recv,
    tap_send,
    tap_recv,
):
    f32, bf16 = jnp.float32, jnp.bfloat16
    data, me = lax.axis_index("dp"), lax.axis_index("seq")
    group = math.isqrt(data_size)
    far, near = data // group, lax.rem(data, group)
    rows_here = qkv_ref.shape[0]
    time_rows = rows_here * size
    taps = cw_ref.shape[0]
    margin = (taps - 1) // 2
    part = qkv_ref.shape[1] // 3 // size
    width = part * size
    tiles = part // LANES
    slots = cot.shape[1]
    scale = head_size ** (-0.5)
    to = [lax.rem(me + k, size) for k in range(size)]
    far_order = [0]
    for k in range(1, group // 2 + 1):
        far_order += [k, group - k] if 2 * k < group else [k]

    def partners(e, body):
        for z in far_order:
            for m in range(size):
                call = functools.partial(
                    body, lax.rem(far + z, group) * group + lax.rem(near + e, group), m
                )
                if z or m:
                    call()
                else:
                    pl.when(e > 0)(call)

    def loop(first, last, body):
        def step(e, carry):
            body(e)
            return carry

        lax.fori_loop(first, last, step, 0)

    def remote(src, dst, send, recv, dp, seq):
        return pltpu.make_async_remote_copy(
            src_ref=src,
            dst_ref=dst,
            send_sem=send,
            recv_sem=recv,
            device_id={"dp": dp, "seq": seq},
            device_id_type=MESH,
        )

    barrier_sem = pltpu.get_barrier_semaphore()

    def greet(dp, m):
        pl.semaphore_signal(
            barrier_sem, inc=1, device_id={"dp": dp, "seq": to[m]}, device_id_type=MESH
        )

    loop(0, group, lambda e: partners(e, greet))

    def part_cols(p, d):
        return pl.ds(pl.multiple_of(p * width + d * part, part), part)

    slot = me * data_size + data
    moves = [(seg_ref.at[0], seg_all.at[me])]
    moves.append((sent_ref.at[data, :, part_cols(0, me)], cot.at[slot]))
    for p in range(3):
        moves.append(
            (qkv_ref.at[:, part_cols(p, me)], mine.at[rows(me, rows_here), pl.ds(p * part, part)])
        )
    own = [pltpu.make_async_copy(src, dst, own_sem.at[n]) for n, (src, dst) in enumerate(moves)]
    for copy in own:
        copy.start()
    clear(shifted.at[0])
    clear(att_pad)
    clear(dk)
    clear(dv)
    pl.semaphore_wait(barrier_sem, data_size * size - 1)

    def seg_copy(k):
        return remote(
            seg_ref.at[0], seg_all.at[me], seq_send.at[k - 1, 3], seq_recv.at[k - 1, 3], data, to[k]
        )

    def seq_copy(k, p, first, count):
        return remote(
            qkv_ref.at[pl.ds(first, count), part_cols(p, to[k])],
            mine.at[pl.ds(pl.multiple_of(me * rows_here + first, SLICE), count), pl.ds(p * part, part)],
            seq_send.at[k - 1, p],
            seq_recv.at[k - 1, p],
            data,
            to[k],
        )

    def in_copy(dp, m):
        remote(
            sent_ref.at[dp, :, part_cols(0, to[m])], cot.at[slot], in_send.at[m], in_recv.at[m], dp, to[m]
        ).start()

    for k in range(1, size):
        seg_copy(k).start()

    def begin(e):
        for k in range(1, size):
            for p in range(3):
                seq_copy(k, p, pl.multiple_of(e * SLICE, SLICE), SLICE).start()
        partners(e, in_copy)

    loop(0, group, begin)
    early = group * SLICE
    for p in range(3):
        for k in range(1, size):
            seq_copy(k, p, early, rows_here - early).start()

    for copy in own:
        copy.wait()
    for k in range(1, size):
        seg_copy(k).wait()
    for m in range(size):
        got = sent_ref.at[pl.ds(0, data_size if m else data_size - 1), :, pl.ds(0, part)]
        pltpu.make_async_copy(got, got, in_send.at[m]).wait()
        pltpu.make_async_copy(got, got, in_recv.at[m]).wait()

    def cols_of(j):
        return pl.ds(pl.multiple_of(me * part + j * LANES, LANES), LANES)

    convolve(time_rows, tiles, taps, cols_of, cot, seg_all, cw_ref, seg_row, labb, shifted, grad_pad, do_t)
    for k in range(1, size):
        for p in range(3):
            seq_copy(k, p, 0, rows_here).wait()
    attend(
        time_rows, part, head_size, mine, seg_row, labb, k_t, v_t, do_t, att_t, dq_t, dk, dv, scores, probs
    )

    def results(c):
        here, there = rows(c, CH), rows(c, CH // slots)
        for j in range(tiles):
            cols = pl.ds(j * LANES, LANES)
            for p, val in enumerate(
                ((dq_t[cols, here] * scale).T, dk[here, cols] * scale, dv[here, cols])
            ):
                stage[there, :, pl.ds(p * part + j * LANES, LANES)] = val.reshape(
                    CH // slots, slots, LANES
                ).astype(bf16)

    chunks(time_rows // CH, results)

    def out_cols(p):
        return pl.ds(pl.multiple_of((p * size + me) * part, part), part)

    def out_copy(dp, m):
        for p in range(3):
            remote(
                stage.at[to[m] * data_size + dp, :, pl.ds(p * part, part)],
                out_ref.at[data, :, out_cols(p)],
                out_send.at[m, p],
                out_recv.at[m, p],
                dp,
                to[m],
            ).start()

    def leave(e):
        partners(e, out_copy)

    loop(0, group // 2, leave)
    own = [
        pltpu.make_async_copy(
            stage.at[slot, :, pl.ds(p * part, part)], out_ref.at[data, :, out_cols(p)], own_sem.at[p]
        )
        for p in range(3)
    ]
    for copy in own:
        copy.start()

    spread_rows(
        lambda c, j: att_t[pl.ds(j * LANES, LANES), rows(c, CH)].T, labb, att_pad, time_rows, 0, tiles
    )
    inner = time_rows + GAP * (SEGMENTS - 1)
    each = terms.shape[1]
    terms[group - 1] = jnp.zeros(terms.shape[1:], f32)
    for j in range(tiles):
        cols = pl.ds(j * LANES, LANES)

        def tap_step(c, sums):
            att = att_pad[rows(c, 8), cols]
            return tuple(
                sums[w] + att * tap_view(shifted, margin, w, c * 8, 8, cols) for w in range(taps)
            )

        sums = lax.fori_loop(
            0, inner // 8, tap_step, tuple(jnp.zeros((8, LANES), f32) for _ in range(taps))
        )
        for w in range(taps):
            terms[w // each, w % each : w % each + 1, cols] = jnp.sum(sums[w], axis=0, keepdims=True)

    near_to = [lax.rem(near + k, group) for k in range(group)]
    far_to = [lax.rem(far + k, group) for k in range(group)]
    used = [0]

    def tap_copy(src, dst, z, n, m):
        i = used[0]
        used[0] += 1
        copy = remote(src, dst, tap_send.at[i], tap_recv.at[i], z * group + n, to[m])
        copy.start()
        return copy

    copies = [
        tap_copy(terms.at[near_to[k]], near_sum.at[k - 1], far, near_to[k], 0) for k in range(1, group)
    ]
    loop(group // 2, group - 2, leave)
    for copy in copies:
        copy.wait()
    total = terms[near]
    for k in range(1, group):
        total = total + near_sum[k - 1]
    far_sum[far] = total
    copies = [tap_copy(far_sum.at[far], far_sum.at[far], far_to[k], near, 0) for k in range(1, group)]
    loop(group - 2, group, leave)
    for copy in copies:
        copy.wait()
    total = far_sum[0]
    for k in range(1, group):
        total = total + far_sum[k]
    whole[me, near] = total * factor
    copies = [
        tap_copy(whole.at[me, near], whole.at[me, near], far, near_to[k], m)
        for k in range(group)
        for m in range(size)
        if k or m
    ]
    for copy in copies:
        copy.wait()
    taps_ref[...] = whole[...]

    for copy in own:
        copy.wait()
    for m in range(size):
        for p in range(3):
            got = out_ref.at[pl.ds(0, data_size if m else data_size - 1), :, pl.ds(0, part)]
            pltpu.make_async_copy(got, got, out_send.at[m, p]).wait()
            pltpu.make_async_copy(got, got, out_recv.at[m, p]).wait()


VMEM = pl.BlockSpec(memory_space=pltpu.VMEM)
ANY = pl.BlockSpec(memory_space=pl.ANY)


def run_block(qkv, sent, seg, cw, data_size, size, head_size, factor):
    f32, bf16 = jnp.float32, jnp.bfloat16
    rows_here, columns = qkv.shape
    taps = cw.shape[0]
    slots = sent.shape[1]
    time_rows, width = rows_here * size, columns // 3 // size
    inner = -(-(time_rows + GAP * (SEGMENTS - 1)) // 96) * 96
    rows_all = inner + 48 + 8
    group = math.isqrt(data_size)
    piece = (group, (taps + 1) // group, width)
    sends = 2 * (group - 1) + group * size - 1
    dma = pltpu.SemaphoreType.DMA
    return pl.pallas_call(
        functools.partial(block_kernel, data_size, size, head_size, factor),
        out_shape=(
            jax.ShapeDtypeStruct((data_size, slots, columns), bf16),
            jax.ShapeDtypeStruct((size,) + piece, f32),
        ),
        in_specs=[ANY, ANY, ANY, VMEM],
        out_specs=(ANY, VMEM),
        scratch_shapes=[
            pltpu.VMEM((size, 1, rows_here), seg.dtype),
            pltpu.VMEM((time_rows, 3 * width), bf16),
            pltpu.VMEM((data_size * size, slots, width), bf16),
            pltpu.VMEM((data_size * size, slots, 3 * width), bf16),
            pltpu.VMEM((1, time_rows), f32),
            pltpu.VMEM((time_rows, LANES), f32),
            pltpu.VMEM((8, rows_all, width), f32),
            pltpu.VMEM((inner, width), f32),
            pltpu.VMEM((rows_all, width), f32),
            pltpu.VMEM((width, time_rows), bf16),
            pltpu.VMEM((width, time_rows), bf16),
            pltpu.VMEM((width, time_rows), f32),
            pltpu.VMEM((width, time_rows), f32),
            pltpu.VMEM((width, time_rows), f32),
            pltpu.VMEM((time_rows, width), f32),
            pltpu.VMEM((time_rows, width), f32),
            pltpu.VMEM((time_rows, PAIR * TB), f32),
            pltpu.VMEM((time_rows, PAIR * TB), bf16),
            pltpu.VMEM(piece, f32),
            pltpu.VMEM(piece, f32),
            pltpu.VMEM(piece, f32),
            pltpu.VMEM((size,) + piece, f32),
            dma((5,)),
            dma((size - 1, 4)),
            dma((size - 1, 4)),
            dma((size,)),
            dma((size,)),
            dma((size, 3)),
            dma((size, 3)),
            dma((sends,)),
            dma((sends,)),
        ],
        compiler_params=pltpu.CompilerParams(
            collective_id=1, has_side_effects=True, vmem_limit_bytes=58 * 1024 * 1024
        ),
        cost_estimate=pl.CostEstimate(
            flops=14 * time_rows * time_rows * width, bytes_accessed=64 << 20, transcendentals=0
        ),
    )(qkv, sent, seg[None], cw)


def local(qkv, grad_in, counts, segment, conv_weight):
    data_size = lax.axis_size("dp")
    time_size = lax.axis_size("seq")
    width = qkv.shape[2] // 3
    part = width // time_size
    head_size = width // H
    slot_rows = grad_in.shape[2]
    taps = conv_weight.shape[0]

    filled = jnp.arange(slot_rows)[None, :] < counts[0][:, None]
    sent = jnp.where(filled[:, :, None], grad_in[0], jnp.asarray(EMPTY, jnp.bfloat16))
    factor = 1.0 / math.sqrt(data_size * slot_rows)
    grads, total = run_block(
        qkv[0], sent, segment, conv_weight, data_size, time_size, head_size, factor
    )
    total = total.reshape(time_size, taps + 1, part).transpose(1, 0, 2)
    conv_weight_grad = total.reshape(taps + 1, time_size * part)[:taps]
    qkv_grad = grads[None]
    return (qkv_grad, conv_weight_grad)


def solution(mesh):
    in_specs = (
        P("dp", "seq", None),
        P("dp", "seq", None, None),
        P("dp", "seq"),
        P("dp", "seq"),
        P(),
    )
    out_specs = (P("dp", "seq", None, None), P())
    return jax.shard_map(local, mesh=mesh, in_specs=in_specs, out_specs=out_specs, check_vma=False)
```

time: 290 us -> 143 us (0.49)
  waiting for transfers between devices: 103 us -> 0 us
  Pallas kernels: 81.8 us -> 133 us
  starting transfers between devices: 34.1 us -> 0 us
  local copies, waits for them, and re-layouts: 36.8 us -> 5.73 us
  blocking collectives: 28.6 us -> 0 us
    all_to_all x5 -> x0, waiting for transfers between devices: 103 us -> none  [the longest x1 58 us: local(): lax.all_to_all(grads.reshape(data_size * time_size, slot_rows, 3 * part),...]
    pallas_call x1, Pallas kernels: 81.8 us -> 133 us  [run_block(): pl.pallas_call(functools.partial(block_kernel, data_size, size, head_size...]
    all_to_all x5 -> x0, starting transfers between devices: 34.1 us -> none  [the longest x1 15.4 us: local(): lax.all_to_all(sent.reshape(data_size * time_size, slot_rows, part), ('dp...]
    all_to_all x2 -> x0, blocking collectives: 28.6 us -> none  [the longest x1 14.9 us: local(): lax.all_to_all(tap_terms.reshape(data_size, 1, share), 'dp', 0, 0, tiled=...]
    reshape x6 -> x1, local copies, waits for them, and re-layouts: 14.9 us -> 1 us  [local(): total = total.reshape(time_size, taps + 1, part).transpose(1, 0, 2)]
    unnamed x7 -> x3, local copies, waits for them, and re-layouts: 11.5 us -> 4.61 us
    all_to_all x2 -> x0, local copies, waits for them, and re-layouts: 4.11 us -> none  [the longest x1 2.43 us: local(): lax.all_to_all(mine.reshape(time_size, rows_here, 3 * part), 'seq', 0, 0,...]
  transfers between devices with their start and end apart: 5 -> 0, of which waited for: 3 -> 0; matrix products, arithmetic and copies ran while one was open for 7% -> 0% of each run, Pallas kernels for 0% -> 0%
where the time goes in v4:
time: 143 us
  Pallas kernels  133 us (93%)
  local copies, waits for them, and re-layouts  5.73 us (4%)
  other arithmetic  3.17 us (2%)
    pallas_call x1, Pallas kernels, run_block(): pl.pallas_call(functools.partial(block_kernel, data_size, size, head_size...  133 us
    unnamed x3, local copies, waits for them, and re-layouts  4.61 us

profile of v4, /device:TPU:1, one launch (start us, length us, event | category | flops | bytes accessed | tf_op | source)
XLA Modules:
  0.0 142.5 jit_solution(2804387629733805406)
XLA Ops:
  0.6 0.7 iota_compare_fusion
  1.4 2.4 %bitcast_select_fusion.sent_ref = bf16[64,4,1536]{2,1,0:T(4,128)(2,1)} fusion(bf16[1,64,4,1536]{3,2,1,0:T(4,128)(2,1)} %param.6, pred[64,4]{1,0:T(8,128)(4,1)S(1)} %iota_compare_fusion), kind=kLoop, calls=%fused_computation | loop fusion | flops 393216 | bytes 1573120 | tf_op jit(solution)/shard_map/jit(_where)/select_n | solution.py:591
  3.8 133.0 %shard_map.68 = (bf16[64,4,4608]{2,1,0:T(4,128)(2,1)}, f32[4,8,4,384]{3,2,1,0:T(4,128)}) custom-call(bf16[256,4608]{1,0:T(8,128)(2,1)} %bitcast.16, bf16[64,4,1536]{2,1,0:T(4,128)(2,1)} %bitcast_select_fusion.sent_ref, s32[1,1,256]{2,1,0:T(1,128)} %bitcast.17, f32[31,1536]{1,0:T(8,128)} %cw_ref.1), custom_call_target="tpu_custom_call" | custom-call | flops 5637144576 | bytes 67108864 | tf_op jit(solution)/shard_map/pallas_call | solution.py:531
  136.8 1.0 reshape.33
  137.8 0.1 copy.7
  138.0 0.7 copy.8
  138.7 3.9 %copy.10 = bf16[1,64,4,4608]{3,2,1,0:T(4,128)(2,1)} copy(bf16[1,64,4,4608]{3,2,1,0:T(4,128)(2,1)} %bitcast.11) | data formatting | bytes 4718592
  (1 shorter events, 0.0 us)

commit v5 on v4

v5 whole, which is shorter than its diff:
```python
import functools
import math

import jax
import jax.numpy as jnp
from jax import lax
from jax.experimental import pallas as pl
from jax.experimental.pallas import tpu as pltpu
from jax.sharding import PartitionSpec as P

H = 16

EMPTY = 128.0
EMPTY_ABOVE = 64.0
MASKED = -1e30
LANES = 128
TB = 512
UB = 256
SLICE = 16
PAIR = 2
GAP = 16
SEGMENTS = 4
MESH = pl.DeviceIdType.MESH
CH = 128


def dot(a, b, contract):
    return lax.dot_general(a, b, (contract, ((), ())), preferred_element_type=jnp.float32)


def rows(index, size):
    return pl.ds(pl.multiple_of(index * size, size), size)


def chunks(count, body):
    def step(index, carry):
        body(index)
        return carry

    lax.fori_loop(0, count, step, 0)


def tap_view(shifted, margin, w, r0, size, cols):
    offset = margin - w
    a, b = offset // 8, offset % 8
    return shifted[b, pl.ds(pl.multiple_of(r0 + GAP + 8 * a, 8), size), cols]


def clear(ref):
    def step(c):
        ref[rows(c, 8), :] = jnp.zeros((8, ref.shape[1]), ref.dtype)

    chunks(ref.shape[0] // 8, step)


def spread_rows(value, labb, target, time_rows, shift, tiles):
    def step(c):
        lab = labb[rows(c, CH), :]
        for j in range(tiles):
            val = value(c, j)
            for s in range(SEGMENTS):
                there = pl.ds(pl.multiple_of(c * CH + GAP * (s + shift), GAP), CH)
                target[there, pl.ds(j * LANES, LANES)] += jnp.where(lab == s + 1.0, val, 0.0)

    chunks(time_rows // CH, step)


def convolve(time_rows, tiles, taps, cols_of, cot, seg_ref, cw_ref, seg_row, labb, shifted, grad_pad, do_t):
    f32 = jnp.float32
    margin = (taps - 1) // 2
    slots = cot.shape[1]
    piece = seg_ref.shape[2]
    for s in range(seg_ref.shape[0]):
        seg_row[:, s * piece : (s + 1) * piece] = seg_ref[s].astype(f32)

    def cot_rows(c, j):
        val = cot[rows(c, CH // slots), :, pl.ds(j * LANES, LANES)].astype(f32)
        return val.reshape(CH, LANES)

    def label(c):
        here = rows(c, CH)
        across = jnp.broadcast_to(seg_row[:, here], (CH, CH)).T
        labb[here, :] = jnp.where(cot_rows(c, 0) < EMPTY_ABOVE, across + 1.0, 0.0)

    chunks(time_rows // CH, label)
    spread_rows(cot_rows, labb, shifted.at[0], time_rows, 1, tiles)

    def shift(c):
        r0 = pl.multiple_of(c * 48, 8)
        for j in range(tiles):
            cols = pl.ds(j * LANES, LANES)
            block = shifted[0, pl.ds(r0, 56), cols]
            for b in range(1, 8):
                shifted[b, pl.ds(r0, 48), cols] = block[b : b + 48]

    chunks((shifted.shape[1] - 8) // 48, shift)

    def conv(c):
        r0 = c * 32
        for j in range(tiles):
            cols = pl.ds(j * LANES, LANES)
            total = jnp.zeros((32, LANES), f32)
            for w in range(taps):
                weight = cw_ref[w : w + 1, cols_of(j)]
                total = total + weight * tap_view(shifted, margin, w, r0, 32, cols)
            grad_pad[pl.ds(pl.multiple_of(r0, 16), 32), cols] = total

    chunks(grad_pad.shape[0] // 32, conv)

    def collect(c):
        lab = labb[rows(c, CH), :]
        for j in range(tiles):
            cols = pl.ds(j * LANES, LANES)
            total = jnp.zeros((CH, LANES), f32)
            for s in range(SEGMENTS):
                there = pl.ds(pl.multiple_of(c * CH + GAP * s, GAP), CH)
                total = total + jnp.where(lab == s + 1.0, grad_pad[there, cols], 0.0)
            do_t[cols, rows(c, CH)] = total.T

    chunks(time_rows // CH, collect)


def flip(time_rows, width, tiles, qkv_ref, k_t, v_t):
    def step(c):
        here = rows(c, CH)
        for j in tiles:
            for n, target in ((1, k_t), (2, v_t)):
                block = qkv_ref[here, pl.ds(n * width + j * LANES, LANES)]
                target[pl.ds(j * LANES, LANES), here] = block.T

    chunks(time_rows // CH, step)


def attend(
    h0, time_rows, width, head_size, qkv_ref, seg_row, labb, k_t, v_t, do_t, att_t, dq_t, dk, dv, scores, probs
):
    f32, bf16 = jnp.float32, jnp.bfloat16
    scale = head_size ** (-0.5)
    cols_here = PAIR * TB
    row_index = lax.broadcasted_iota(jnp.int32, (UB, cols_here), 0)
    col_index = lax.broadcasted_iota(jnp.int32, (UB, cols_here), 1) % TB
    apart = col_index - row_index
    to_exp2 = scale * math.log2(math.e)

    first, last = h0 * head_size, (h0 + PAIR) * head_size
    lane0 = first // LANES * LANES
    span = -(-last // LANES) * LANES - lane0
    lane = lax.broadcasted_iota(jnp.int32, (TB, span), 1) + lane0
    head_rows = [pl.ds((h0 + n) * head_size, head_size) for n in range(PAIR)]

    def beside(values):
        return jnp.concatenate(values, axis=1)

    def time_block(tb, carry):
        here = rows(tb, TB)
        q = qkv_ref[here, pl.ds(lane0, span)]
        q = jnp.concatenate(
            [
                jnp.where(
                    (lane >= (h0 + n) * head_size) & (lane < (h0 + n + 1) * head_size),
                    q,
                    jnp.zeros((), bf16),
                )
                for n in range(PAIR)
            ],
            axis=0,
        )
        want = beside([seg_row[:, here] + 1.0] * PAIR)

        def score_step(ub, highest):
            keys = rows(ub, UB)
            s = dot(qkv_ref[keys, pl.ds(width + lane0, span)], q, ((1,), (1,)))
            lab = beside([labb[keys, :]] * (cols_here // LANES))
            ok = (lab == want) | (apart == ub * UB - tb * TB)
            s = jnp.where(ok, s, MASKED)
            scores[keys, :] = s
            return jnp.maximum(highest, jnp.max(s.reshape(UB // 8, 8, cols_here), axis=0))

        highest = lax.fori_loop(0, time_rows // UB, score_step, jnp.full((8, cols_here), MASKED, f32), unroll=True)
        highest = jnp.max(highest, axis=0, keepdims=True) * to_exp2
        for n in range(PAIR):
            att_t[head_rows[n], here] = jnp.zeros((head_size, TB), f32)
            dq_t[head_rows[n], here] = jnp.zeros((head_size, TB), f32)

        def soft_step(ub, total):
            keys = rows(ub, UB)
            p = jnp.exp2(scores[keys, :] * to_exp2 - highest)
            total = total + jnp.sum(p.reshape(UB // 8, 8, cols_here), axis=0)
            p = p.astype(bf16)
            probs[keys, :] = p
            for n in range(PAIR):
                att_t[head_rows[n], here] += dot(
                    v_t[head_rows[n], keys], p[:, n * TB : (n + 1) * TB], ((1,), (0,))
                )
            return total

        total = lax.fori_loop(0, time_rows // UB, soft_step, jnp.zeros((8, cols_here), f32), unroll=True)
        inverse = 1.0 / jnp.sum(total, axis=0, keepdims=True)
        deltas, wide = [], []
        for n in range(PAIR):
            inv = inverse[:, n * TB : (n + 1) * TB]
            att = (att_t[head_rows[n], here] * inv).astype(bf16).astype(f32)
            att_t[head_rows[n], here] = att
            do = do_t[head_rows[n], here].astype(bf16).astype(f32)
            deltas.append(jnp.sum(do * att, axis=0, keepdims=True) * inv)
            before = (h0 + n) * head_size - lane0
            after = span - before - head_size
            parts = [(do * inv).astype(bf16)]
            if before:
                parts = [jnp.zeros((before, TB), bf16)] + parts
            if after:
                parts = parts + [jnp.zeros((after, TB), bf16)]
            wide.append(jnp.concatenate(parts, axis=0))
        delta, do_wide = beside(deltas), beside(wide)

        def grad_step(ub, carry):
            keys = rows(ub, UB)
            p = probs[keys, :]
            dp = dot(qkv_ref[keys, pl.ds(2 * width + lane0, span)], do_wide, ((1,), (0,)))
            ds = (p.astype(f32) * (dp - delta)).astype(bf16)
            dk[keys, pl.ds(lane0, span)] += dot(ds, q, ((1,), (0,)))
            dv[keys, pl.ds(lane0, span)] += dot(p, do_wide, ((1,), (1,)))
            for n in range(PAIR):
                dq_t[head_rows[n], here] += dot(
                    k_t[head_rows[n], keys], ds[:, n * TB : (n + 1) * TB], ((1,), (0,))
                )
            return carry

        lax.fori_loop(0, time_rows // UB, grad_step, 0, unroll=True)
        return carry

    lax.fori_loop(0, time_rows // TB, time_block, 0)


def block_kernel(
    data_size,
    size,
    head_size,
    factor,
    qkv_ref,
    grad_ref,
    counts_ref,
    seg_ref,
    cw_ref,
    out_ref,
    taps_ref,
    seg_all,
    mine,
    sent,
    cot,
    stage,
    seg_row,
    labb,
    shifted,
    grad_pad,
    att_pad,
    k_t,
    v_t,
    do_t,
    att_t,
    dq_t,
    dk,
    dv,
    scores,
    probs,
    terms,
    near_sum,
    far_sum,
    whole,
    own_sem,
    seq_send,
    seq_recv,
    in_send,
    in_recv,
    out_send,
    out_recv,
    tap_send,
    tap_recv,
):
    f32, bf16 = jnp.float32, jnp.bfloat16
    data, me = lax.axis_index("dp"), lax.axis_index("seq")
    group = math.isqrt(data_size)
    far, near = data // group, lax.rem(data, group)
    qkv_ref = qkv_ref.at[0]
    rows_here = qkv_ref.shape[0]
    time_rows = rows_here * size
    taps = cw_ref.shape[0]
    margin = (taps - 1) // 2
    part = qkv_ref.shape[1] // 3 // size
    width = part * size
    tiles = part // LANES
    slots = cot.shape[1]
    scale = head_size ** (-0.5)
    to = [lax.rem(me + k, size) for k in range(size)]
    far_order = [0]
    for k in range(1, group // 2 + 1):
        far_order += [k, group - k] if 2 * k < group else [k]

    def partners(e, body):
        for z in far_order:
            for m in range(size):
                call = functools.partial(
                    body, lax.rem(far + z, group) * group + lax.rem(near + e, group), m
                )
                if z or m:
                    call()
                else:
                    pl.when(e > 0)(call)

    def loop(first, last, body):
        def step(e, carry):
            body(e)
            return carry

        lax.fori_loop(first, last, step, 0)

    def remote(src, dst, send, recv, dp, seq):
        return pltpu.make_async_remote_copy(
            src_ref=src,
            dst_ref=dst,
            send_sem=send,
            recv_sem=recv,
            device_id={"dp": dp, "seq": seq},
            device_id_type=MESH,
        )

    barrier_sem = pltpu.get_barrier_semaphore()

    def greet(dp, m):
        pl.semaphore_signal(
            barrier_sem, inc=1, device_id={"dp": dp, "seq": to[m]}, device_id_type=MESH
        )

    loop(0, group, lambda e: partners(e, greet))

    def part_cols(p, d):
        return pl.ds(pl.multiple_of(p * width + d * part, part), part)

    slot = me * data_size + data
    moves = [(seg_ref.at[0], seg_all.at[me])]
    for p in range(3):
        moves.append(
            (qkv_ref.at[:, part_cols(p, me)], mine.at[rows(me, rows_here), pl.ds(p * part, part)])
        )
    own = [pltpu.make_async_copy(src, dst, own_sem.at[n]) for n, (src, dst) in enumerate(moves)]
    for copy in own:
        copy.start()
    slot_row = lax.broadcasted_iota(jnp.int32, sent.shape[1:], 0)

    def mark_empty(j):
        val = jnp.where(slot_row < counts_ref[0, j], grad_ref[0, j].astype(f32), EMPTY)
        sent[j] = val.astype(bf16)

    chunks(data_size, mark_empty)
    own_cot = pltpu.make_async_copy(sent.at[data, :, part_cols(0, me)], cot.at[slot], own_sem.at[4])
    own_cot.start()
    clear(shifted.at[0])
    clear(att_pad)
    clear(dk)
    clear(dv)
    pl.semaphore_wait(barrier_sem, data_size * size - 1)

    def seg_copy(k):
        return remote(
            seg_ref.at[0], seg_all.at[me], seq_send.at[k - 1, 6], seq_recv.at[k - 1, 6], data, to[k]
        )

    def seq_copy(k, p, half, first, count):
        start, lanes = ((0, 2 * LANES), (2 * LANES, part - 2 * LANES))[half]
        src_col = pl.multiple_of(p * width + to[k] * part + start, LANES)
        return remote(
            qkv_ref.at[pl.ds(first, count), pl.ds(src_col, lanes)],
            mine.at[
                pl.ds(pl.multiple_of(me * rows_here + first, SLICE), count),
                pl.ds(p * part + start, lanes),
            ],
            seq_send.at[k - 1, 3 * half + p],
            seq_recv.at[k - 1, 3 * half + p],
            data,
            to[k],
        )

    def in_copy(dp, m):
        remote(
            sent.at[dp, :, part_cols(0, to[m])], cot.at[slot], in_send.at[m], in_recv.at[m], dp, to[m]
        ).start()

    for k in range(1, size):
        seg_copy(k).start()

    def begin(e):
        for k in range(1, size):
            for p in range(3):
                seq_copy(k, p, 0, pl.multiple_of(e * SLICE, SLICE), SLICE).start()
        partners(e, in_copy)

    loop(0, group, begin)
    early = group * SLICE
    for first, half in ((early, 0), (0, 1)):
        for p in range(3):
            for k in range(1, size):
                seq_copy(k, p, half, first, rows_here - first).start()

    def bytes_of(m, ref):
        got = ref.at[pl.ds(0, data_size if m else data_size - 1)]
        return got, got

    for copy in own + [own_cot]:
        copy.wait()
    for k in range(1, size):
        seg_copy(k).wait()
    for m in range(size):
        pltpu.make_async_copy(*bytes_of(m, out_ref.at[:, 0, pl.ds(0, tiles)]), in_recv.at[m]).wait()

    def cols_of(j):
        return pl.ds(pl.multiple_of(me * part + j * LANES, LANES), LANES)

    convolve(time_rows, tiles, taps, cols_of, cot, seg_all, cw_ref, seg_row, labb, shifted, grad_pad, do_t)
    def results(first, last):
        def step(c):
            here, there = rows(c, CH), rows(c, CH // slots)
            for j in range(first, last):
                cols = pl.ds(j * LANES, LANES)
                for p, val in enumerate(
                    ((dq_t[cols, here] * scale).T, dk[here, cols] * scale, dv[here, cols])
                ):
                    stage[there, p, j] = val.reshape(CH // slots, slots, LANES).astype(bf16)

        chunks(time_rows // CH, step)

    def out_pair(index, half):
        if half == 0:
            return stage.at[index, :, 0], out_ref.at[data, :, me * tiles]
        here = pl.ds(1, tiles - 1)
        return stage.at[index, :, here], out_ref.at[data, :, pl.ds(me * tiles + 1, tiles - 1)]

    def leave(half):
        def copy(dp, m):
            src, dst = out_pair(to[m] * data_size + dp, half)
            remote(src, dst, out_send.at[m, half], out_recv.at[m, half], dp, to[m]).start()

        return lambda e: partners(e, copy)

    def own_out(half):
        copy = pltpu.make_async_copy(*out_pair(slot, half), own_sem.at[half])
        copy.start()
        return copy

    for half in range(2):
        for k in range(1, size):
            for p in range(3):
                seq_copy(k, p, half, 0, rows_here).wait_recv()
        flip(time_rows, part, ((0, 1), (2,))[half], mine, k_t, v_t)
        attend(
            half * PAIR,
            time_rows,
            part,
            head_size,
            mine,
            seg_row,
            labb,
            k_t,
            v_t,
            do_t,
            att_t,
            dq_t,
            dk,
            dv,
            scores,
            probs,
        )
        if half == 0:
            results(0, 1)
            own = [own_out(0)]
            loop(0, group, leave(0))
        else:
            results(1, tiles)
            own.append(own_out(1))
            loop(0, group // 2, leave(1))

    spread_rows(
        lambda c, j: att_t[pl.ds(j * LANES, LANES), rows(c, CH)].T, labb, att_pad, time_rows, 0, tiles
    )
    inner = time_rows + GAP * (SEGMENTS - 1)
    each = terms.shape[1]
    terms[group - 1] = jnp.zeros(terms.shape[1:], f32)
    for j in range(tiles):
        cols = pl.ds(j * LANES, LANES)

        def tap_step(c, sums):
            att = att_pad[rows(c, 8), cols]
            return tuple(
                sums[w] + att * tap_view(shifted, margin, w, c * 8, 8, cols) for w in range(taps)
            )

        sums = lax.fori_loop(
            0, inner // 8, tap_step, tuple(jnp.zeros((8, LANES), f32) for _ in range(taps))
        )
        for w in range(taps):
            terms[w // each, w % each : w % each + 1, cols] = jnp.sum(sums[w], axis=0, keepdims=True)

    near_to = [lax.rem(near + k, group) for k in range(group)]
    far_to = [lax.rem(far + k, group) for k in range(group)]
    used = [0]

    def tap_copy(src, dst, z, n, m):
        i = used[0]
        used[0] += 1
        copy = remote(src, dst, tap_send.at[i], tap_recv.at[i], z * group + n, to[m])
        copy.start()
        return copy

    copies = [
        tap_copy(terms.at[near_to[k]], near_sum.at[k - 1], far, near_to[k], 0) for k in range(1, group)
    ]
    loop(group // 2, group - 2, leave(1))
    for copy in copies:
        copy.wait()
    total = terms[near]
    for k in range(1, group):
        total = total + near_sum[k - 1]
    far_sum[far] = total
    copies = [tap_copy(far_sum.at[far], far_sum.at[far], far_to[k], near, 0) for k in range(1, group)]
    loop(group - 2, group, leave(1))
    for copy in copies:
        copy.wait()
    total = far_sum[0]
    for k in range(1, group):
        total = total + far_sum[k]
    whole[me, near] = total * factor
    copies = [
        tap_copy(whole.at[me, near], whole.at[me, near], far, near_to[k], m)
        for k in range(group)
        for m in range(size)
        if k or m
    ]
    for copy in copies:
        copy.wait()
    for m in range(size):
        for g in range(group):
            count = min(each, taps - g * each)
            taps_ref[g * each : g * each + count, m * part : (m + 1) * part] = whole[m, g, :count]

    for copy in own:
        copy.wait()
    for k in range(1, size):
        for p in range(3):
            for half in range(2):
                seq_copy(k, p, half, 0, rows_here).wait_send()
    for m in range(size):
        pltpu.make_async_copy(*bytes_of(m, out_ref.at[:, 0, pl.ds(0, tiles)]), in_send.at[m]).wait()
        for half, ref in enumerate((out_ref.at[:, :, 0], out_ref.at[:, :, pl.ds(0, tiles - 1)])):
            pltpu.make_async_copy(*bytes_of(m, ref), out_send.at[m, half]).wait()
            pltpu.make_async_copy(*bytes_of(m, ref), out_recv.at[m, half]).wait()


VMEM = pl.BlockSpec(memory_space=pltpu.VMEM)
ANY = pl.BlockSpec(memory_space=pl.ANY)


def run_block(qkv, grad_in, counts, seg, cw, data_size, size, head_size, factor):
    f32, bf16 = jnp.float32, jnp.bfloat16
    _, rows_here, columns = qkv.shape
    taps = cw.shape[0]
    slots = grad_in.shape[2]
    time_rows, width = rows_here * size, columns // 3 // size
    tiles = width // LANES
    inner = -(-(time_rows + GAP * (SEGMENTS - 1)) // 96) * 96
    rows_all = inner + 48 + 8
    group = math.isqrt(data_size)
    piece = (group, (taps + 1) // group, width)
    sends = 2 * (group - 1) + group * size - 1
    dma = pltpu.SemaphoreType.DMA
    return pl.pallas_call(
        functools.partial(block_kernel, data_size, size, head_size, factor),
        out_shape=(
            jax.ShapeDtypeStruct((data_size, 3, size * tiles, slots, LANES), bf16),
            jax.ShapeDtypeStruct((taps, width * size), f32),
        ),
        in_specs=[ANY, VMEM, pl.BlockSpec(memory_space=pltpu.SMEM), ANY, VMEM],
        out_specs=(ANY, VMEM),
        scratch_shapes=[
            pltpu.VMEM((size, 1, rows_here), seg.dtype),
            pltpu.VMEM((time_rows, 3 * width), bf16),
            pltpu.VMEM((data_size, slots, size * width), bf16),
            pltpu.VMEM((data_size * size, slots, width), bf16),
            pltpu.VMEM((data_size * size, 3, tiles, slots, LANES), bf16),
            pltpu.VMEM((1, time_rows), f32),
            pltpu.VMEM((time_rows, LANES), f32),
            pltpu.VMEM((8, rows_all, width), f32),
            pltpu.VMEM((inner, width), f32),
            pltpu.VMEM((rows_all, width), f32),
            pltpu.VMEM((width, time_rows), bf16),
            pltpu.VMEM((width, time_rows), bf16),
            pltpu.VMEM((width, time_rows), f32),
            pltpu.VMEM((width, time_rows), f32),
            pltpu.VMEM((width, time_rows), f32),
            pltpu.VMEM((time_rows, width), f32),
            pltpu.VMEM((time_rows, width), f32),
            pltpu.VMEM((time_rows, PAIR * TB), f32),
            pltpu.VMEM((time_rows, PAIR * TB), bf16),
            pltpu.VMEM(piece, f32),
            pltpu.VMEM(piece, f32),
            pltpu.VMEM(piece, f32),
            pltpu.VMEM((size,) + piece, f32),
            dma((5,)),
            dma((size - 1, 7)),
            dma((size - 1, 7)),
            dma((size,)),
            dma((size,)),
            dma((size, 2)),
            dma((size, 2)),
            dma((sends,)),
            dma((sends,)),
        ],
        compiler_params=pltpu.CompilerParams(
            collective_id=1, has_side_effects=True, vmem_limit_bytes=58 * 1024 * 1024
        ),
        cost_estimate=pl.CostEstimate(
            flops=14 * time_rows * time_rows * width, bytes_accessed=64 << 20, transcendentals=0
        ),
    )(qkv, grad_in, counts, seg[None], cw)


def local(qkv, grad_in, counts, segment, conv_weight):
    data_size = lax.axis_size("dp")
    time_size = lax.axis_size("seq")
    width = qkv.shape[2] // 3
    head_size = width // H
    slot_rows = grad_in.shape[2]

    factor = 1.0 / math.sqrt(data_size * slot_rows)
    grads, conv_weight_grad = run_block(
        qkv, grad_in, counts, segment, conv_weight, data_size, time_size, head_size, factor
    )
    qkv_grad = grads.transpose(0, 3, 1, 2, 4).reshape(1, data_size, slot_rows, 3 * width)
    return (qkv_grad, conv_weight_grad)


def solution(mesh):
    in_specs = (
        P("dp", "seq", None),
        P("dp", "seq", None, None),
        P("dp", "seq"),
        P("dp", "seq"),
        P(),
    )
    out_specs = (P("dp", "seq", None, None), P())
    return jax.shard_map(local, mesh=mesh, in_specs=in_specs, out_specs=out_specs, check_vma=False)
```

time: 143 us -> 120 us (0.84)
  Pallas kernels: 133 us -> 115 us
  other arithmetic: 3.17 us -> 0 us
    pallas_call x1, Pallas kernels: 133 us -> 115 us  [run_block(): pl.pallas_call(functools.partial(block_kernel, data_size, size, head_size...]
    select_n x1 -> x0, other arithmetic: 2.44 us -> none  [local(): jnp.where(filled[:, :, None], grad_in[0], jnp.asarray(EMPTY, jnp.bfloat16))]
    unnamed x3 -> x4, local copies, waits for them, and re-layouts: 4.61 us -> 4.6 us
where the time goes in v5:
time: 120 us
  Pallas kernels  115 us (96%)
  local copies, waits for them, and re-layouts  4.6 us (4%)
    pallas_call x1, Pallas kernels, run_block(): pl.pallas_call(functools.partial(block_kernel, data_size, size, head_size...  115 us
    unnamed x4, local copies, waits for them, and re-layouts  4.6 us

profile of v5, /device:TPU:1, one launch (start us, length us, event | category | flops | bytes accessed | tf_op | source)
XLA Modules:
  0.0 120.1 jit_solution(17156670990368077854)
XLA Ops:
  0.6 114.8 %shard_map.68 = (bf16[64,3,12,4,128]{4,3,2,1,0:T(4,128)(2,1)}, f32[31,1536]{1,0:T(8,128)}) custom-call(bf16[1,256,4608]{2,1,0:T(8,128)(2,1)} %qkv_ref.1, bf16[1,64,4,1536]{3,2,1,0:T(4,128)(2,1)} %grad_ref.1, s32[1,64]{1,0:T(1,128)} %counts_ref.1, s32[1,1,256]{2,1,0:T(1,128)} %bitcast.5, f32[31,1536]{1,0:T(8,128)} %cw_ref.1), custom_call_target="tpu_custom_call" | custom-call | flops 5637144576 | bytes 67108864 | tf_op jit(solution)/shard_map/pallas_call | solution.py:574
  115.5 0.0 copy-start
  115.5 3.9 %copy.9 = bf16[1,64,4,4608]{3,2,1,0:T(4,128)(2,1)} copy(bf16[1,64,4,4608]{3,2,1,0:T(4,128)(2,1)} %bitcast.4) | data formatting | bytes 4718592
  119.4 0.0 copy-done
  119.4 0.7 copy.10
Async XLA Ops:
  115.5 3.9 %copy-start = (f32[31,1536]{1,0:T(8,128)S(1)}, f32[31,1536]{1,0:T(8,128)}, u32[]{:S(2)}) copy-start(f32[31,1536]{1,0:T(8,128)} %get-tuple-element.9) | copy-start | bytes 571396

commit v6 on v5

--- a/solution.py
+++ b/solution.py
@@ -17,6 +17,7 @@
 TB = 512
 UB = 256
 SLICE = 16
+CONV = 64
 PAIR = 2
 GAP = 16
 SEGMENTS = 4
@@ -56,7 +57,7 @@
 def spread_rows(value, labb, target, time_rows, shift, tiles):
     def step(c):
         lab = labb[rows(c, CH), :]
-        for j in range(tiles):
+        for j in tiles:
             val = value(c, j)
             for s in range(SEGMENTS):
                 there = pl.ds(pl.multiple_of(c * CH + GAP * (s + shift), GAP), CH)
@@ -65,17 +66,10 @@
     chunks(time_rows // CH, step)
 
 
-def convolve(time_rows, tiles, taps, cols_of, cot, seg_ref, cw_ref, seg_row, labb, shifted, grad_pad, do_t):
-    f32 = jnp.float32
-    margin = (taps - 1) // 2
-    slots = cot.shape[1]
+def label_rows(time_rows, cot_rows, seg_ref, seg_row, labb):
     piece = seg_ref.shape[2]
     for s in range(seg_ref.shape[0]):
-        seg_row[:, s * piece : (s + 1) * piece] = seg_ref[s].astype(f32)
-
-    def cot_rows(c, j):
-        val = cot[rows(c, CH // slots), :, pl.ds(j * LANES, LANES)].astype(f32)
-        return val.reshape(CH, LANES)
+        seg_row[:, s * piece : (s + 1) * piece] = seg_ref[s].astype(jnp.float32)
 
     def label(c):
         here = rows(c, CH)
@@ -83,11 +77,16 @@
         labb[here, :] = jnp.where(cot_rows(c, 0) < EMPTY_ABOVE, across + 1.0, 0.0)
 
     chunks(time_rows // CH, label)
+
+
+def convolve(time_rows, tiles, taps, cols_of, cot_rows, cw_ref, labb, shifted, grad_pad, do_t):
+    f32 = jnp.float32
+    margin = (taps - 1) // 2
     spread_rows(cot_rows, labb, shifted.at[0], time_rows, 1, tiles)
 
     def shift(c):
         r0 = pl.multiple_of(c * 48, 8)
-        for j in range(tiles):
+        for j in tiles:
             cols = pl.ds(j * LANES, LANES)
             block = shifted[0, pl.ds(r0, 56), cols]
             for b in range(1, 8):
@@ -96,26 +95,30 @@
     chunks((shifted.shape[1] - 8) // 48, shift)
 
     def conv(c):
-        r0 = c * 32
-        for j in range(tiles):
+        r0 = pl.multiple_of(c * CONV, CONV)
+        for j in tiles:
             cols = pl.ds(j * LANES, LANES)
-            total = jnp.zeros((32, LANES), f32)
-            for w in range(taps):
-                weight = cw_ref[w : w + 1, cols_of(j)]
-                total = total + weight * tap_view(shifted, margin, w, r0, 32, cols)
-            grad_pad[pl.ds(pl.multiple_of(r0, 16), 32), cols] = total
-
-    chunks(grad_pad.shape[0] // 32, conv)
+            total = jnp.zeros((CONV, LANES), f32)
+            for b in range(8):
+                block = shifted[b, pl.ds(r0, CONV + 2 * GAP - 8), cols]
+                for a in range(-2, 2):
+                    w = margin - 8 * a - b
+                    if 0 <= w < taps:
+                        weight = cw_ref[w : w + 1, cols_of(j)]
+                        total = total + weight * block[GAP + 8 * a : GAP + 8 * a + CONV]
+            grad_pad[pl.ds(r0, CONV), cols] = total
+
+    chunks(grad_pad.shape[0] // CONV, conv)
 
     def collect(c):
         lab = labb[rows(c, CH), :]
-        for j in range(tiles):
+        for j in tiles:
             cols = pl.ds(j * LANES, LANES)
             total = jnp.zeros((CH, LANES), f32)
             for s in range(SEGMENTS):
                 there = pl.ds(pl.multiple_of(c * CH + GAP * s, GAP), CH)
                 total = total + jnp.where(lab == s + 1.0, grad_pad[there, cols], 0.0)
-            do_t[cols, rows(c, CH)] = total.T
+            do_t[cols, rows(c, CH)] = total.astype(jnp.bfloat16).T
 
     chunks(time_rows // CH, collect)
 
@@ -201,7 +204,7 @@
             inv = inverse[:, n * TB : (n + 1) * TB]
             att = (att_t[head_rows[n], here] * inv).astype(bf16).astype(f32)
             att_t[head_rows[n], here] = att
-            do = do_t[head_rows[n], here].astype(bf16).astype(f32)
+            do = do_t[head_rows[n], here].astype(f32)
             deltas.append(jnp.sum(do * att, axis=0, keepdims=True) * inv)
             before = (h0 + n) * head_size - lane0
             after = span - before - head_size
@@ -238,14 +241,16 @@
     head_size,
     factor,
     qkv_ref,
-    grad_ref,
+    grad_in_ref,
     counts_ref,
     seg_ref,
-    cw_ref,
+    weights_ref,
     out_ref,
     taps_ref,
     seg_all,
     mine,
+    grad_ref,
+    cw_ref,
     sent,
     cot,
     stage,
@@ -267,6 +272,7 @@
     near_sum,
     far_sum,
     whole,
+    all_in,
     own_sem,
     seq_send,
     seq_recv,
@@ -294,18 +300,17 @@
     to = [lax.rem(me + k, size) for k in range(size)]
     far_order = [0]
     for k in range(1, group // 2 + 1):
-        far_order += [k, group - k] if 2 * k < group else [k]
+        far_order = ([k, group - k] if 2 * k < group else [k]) + far_order
 
     def partners(e, body):
-        for z in far_order:
-            for m in range(size):
-                call = functools.partial(
-                    body, lax.rem(far + z, group) * group + lax.rem(near + e, group), m
-                )
+        for m in range(size):
+            for z in far_order:
                 if z or m:
-                    call()
-                else:
-                    pl.when(e > 0)(call)
+                    body(lax.rem(far + z, group) * group + lax.rem(near + e, group), m)
+
+    def neighbours(body):
+        for k in range(1, group):
+            body(far * group + lax.rem(near + k, group), 0)
 
     def loop(first, last, body):
         def step(e, carry):
@@ -331,20 +336,27 @@
             barrier_sem, inc=1, device_id={"dp": dp, "seq": to[m]}, device_id_type=MESH
         )
 
-    loop(0, group, lambda e: partners(e, greet))
+    across = [(z, m) for z in range(group) for m in range(size) if z or m]
+    neighbours(greet)
+    for z, m in across:
+        greet(lax.rem(far + z, group) * group + near, m)
 
     def part_cols(p, d):
         return pl.ds(pl.multiple_of(p * width + d * part, part), part)
 
     slot = me * data_size + data
+    grad_copy = pltpu.make_async_copy(grad_in_ref, grad_ref, own_sem.at[5])
+    grad_copy.start()
     moves = [(seg_ref.at[0], seg_all.at[me])]
     for p in range(3):
         moves.append(
             (qkv_ref.at[:, part_cols(p, me)], mine.at[rows(me, rows_here), pl.ds(p * part, part)])
         )
+    moves.append((weights_ref, cw_ref))
     own = [pltpu.make_async_copy(src, dst, own_sem.at[n]) for n, (src, dst) in enumerate(moves)]
     for copy in own:
         copy.start()
+    grad_copy.wait()
     slot_row = lax.broadcasted_iota(jnp.int32, sent.shape[1:], 0)
 
     def mark_empty(j):
@@ -352,13 +364,22 @@
         sent[j] = val.astype(bf16)
 
     chunks(data_size, mark_empty)
-    own_cot = pltpu.make_async_copy(sent.at[data, :, part_cols(0, me)], cot.at[slot], own_sem.at[4])
+    own_cot = pltpu.make_async_copy(sent.at[data, :, part_cols(0, me)], cot.at[slot], own_sem.at[6])
     own_cot.start()
     clear(shifted.at[0])
     clear(att_pad)
     clear(dk)
     clear(dv)
-    pl.semaphore_wait(barrier_sem, data_size * size - 1)
+    pl.semaphore_wait(barrier_sem, group - 1 + len(across))
+    for z, m in across:
+        pl.semaphore_signal(
+            all_in,
+            inc=1,
+            device_id={"dp": lax.rem(far + z, group) * group + near, "seq": to[m]},
+            device_id_type=MESH,
+        )
+
+    halves = ((0, 2 * LANES), (2 * LANES, part - 2 * LANES))
 
     def seg_copy(k):
         return remote(
@@ -366,7 +387,7 @@
         )
 
     def seq_copy(k, p, half, first, count):
-        start, lanes = ((0, 2 * LANES), (2 * LANES, part - 2 * LANES))[half]
+        start, lanes = halves[half]
         src_col = pl.multiple_of(p * width + to[k] * part + start, LANES)
         return remote(
             qkv_ref.at[pl.ds(first, count), pl.ds(src_col, lanes)],
@@ -380,26 +401,43 @@
             to[k],
         )
 
-    def in_copy(dp, m):
-        remote(
-            sent.at[dp, :, part_cols(0, to[m])], cot.at[slot], in_send.at[m], in_recv.at[m], dp, to[m]
-        ).start()
+    def in_copy(half):
+        start, lanes = halves[half]
+
+        def copy(dp, m):
+            src_col = pl.multiple_of(to[m] * part + start, LANES)
+            remote(
+                sent.at[dp, :, pl.ds(src_col, lanes)],
+                cot.at[slot, :, pl.ds(start, lanes)],
+                in_send.at[m, half],
+                in_recv.at[m, half],
+                dp,
+                to[m],
+            ).start()
+
+        return copy
 
     for k in range(1, size):
         seg_copy(k).start()
 
-    def begin(e):
+    pl.semaphore_wait(all_in, len(across))
+
+    def begin(half, slice_rows):
+        def step(e):
+            for k in range(1, size):
+                for p in range(3):
+                    first = pl.multiple_of(e * slice_rows, slice_rows)
+                    seq_copy(k, p, half, first, slice_rows).start()
+            partners(e, in_copy(half))
+
+        loop(0, group, step)
+        neighbours(in_copy(half))
+
+    begin(0, SLICE)
+    early = group * SLICE
+    for p in range(3):
         for k in range(1, size):
-            for p in range(3):
-                seq_copy(k, p, 0, pl.multiple_of(e * SLICE, SLICE), SLICE).start()
-        partners(e, in_copy)
-
-    loop(0, group, begin)
-    early = group * SLICE
-    for first, half in ((early, 0), (0, 1)):
-        for p in range(3):
-            for k in range(1, size):
-                seq_copy(k, p, half, first, rows_here - first).start()
+            seq_copy(k, p, 0, early, rows_here - early).start()
 
     def bytes_of(m, ref):
         got = ref.at[pl.ds(0, data_size if m else data_size - 1)]
@@ -409,13 +447,16 @@
         copy.wait()
     for k in range(1, size):
         seg_copy(k).wait()
-    for m in range(size):
-        pltpu.make_async_copy(*bytes_of(m, out_ref.at[:, 0, pl.ds(0, tiles)]), in_recv.at[m]).wait()
+    def in_bytes(m, half):
+        return bytes_of(m, out_ref.at[:, 0, pl.ds(0, halves[half][1] // LANES)])
 
     def cols_of(j):
         return pl.ds(pl.multiple_of(me * part + j * LANES, LANES), LANES)
 
-    convolve(time_rows, tiles, taps, cols_of, cot, seg_all, cw_ref, seg_row, labb, shifted, grad_pad, do_t)
+    def cot_rows(c, j):
+        val = cot[rows(c, CH // slots), :, pl.ds(j * LANES, LANES)].astype(f32)
+        return val.reshape(CH, LANES)
+
     def results(first, last):
         def step(c):
             here, there = rows(c, CH), rows(c, CH // slots)
@@ -439,7 +480,7 @@
             src, dst = out_pair(to[m] * data_size + dp, half)
             remote(src, dst, out_send.at[m, half], out_recv.at[m, half], dp, to[m]).start()
 
-        return lambda e: partners(e, copy)
+        return copy, lambda e: partners(e, copy)
 
     def own_out(half):
         copy = pltpu.make_async_copy(*out_pair(slot, half), own_sem.at[half])
@@ -447,10 +488,18 @@
         return copy
 
     for half in range(2):
+        new = ((0, 1), (2,))[half]
+        for m in range(size):
+            pltpu.make_async_copy(*in_bytes(m, half), in_recv.at[m, half]).wait()
+        if half == 0:
+            label_rows(time_rows, cot_rows, seg_all, seg_row, labb)
+        convolve(time_rows, new, taps, cols_of, cot_rows, cw_ref, labb, shifted, grad_pad, do_t)
         for k in range(1, size):
             for p in range(3):
                 seq_copy(k, p, half, 0, rows_here).wait_recv()
-        flip(time_rows, part, ((0, 1), (2,))[half], mine, k_t, v_t)
+        if half == 0:
+            begin(1, rows_here // group)
+        flip(time_rows, part, new, mine, k_t, v_t)
         attend(
             half * PAIR,
             time_rows,
@@ -472,14 +521,16 @@
         if half == 0:
             results(0, 1)
             own = [own_out(0)]
-            loop(0, group, leave(0))
+            neighbours(leave(0)[0])
+            loop(0, group, leave(0)[1])
         else:
             results(1, tiles)
             own.append(own_out(1))
-            loop(0, group // 2, leave(1))
+            neighbours(leave(1)[0])
+            loop(0, group // 2, leave(1)[1])
 
     spread_rows(
-        lambda c, j: att_t[pl.ds(j * LANES, LANES), rows(c, CH)].T, labb, att_pad, time_rows, 0, tiles
+        lambda c, j: att_t[pl.ds(j * LANES, LANES), rows(c, CH)].T, labb, att_pad, time_rows, 0, range(tiles)
     )
     inner = time_rows + GAP * (SEGMENTS - 1)
     each = terms.shape[1]
@@ -513,7 +564,7 @@
     copies = [
         tap_copy(terms.at[near_to[k]], near_sum.at[k - 1], far, near_to[k], 0) for k in range(1, group)
     ]
-    loop(group // 2, group - 2, leave(1))
+    loop(group // 2, group - 2, leave(1)[1])
     for copy in copies:
         copy.wait()
     total = terms[near]
@@ -521,7 +572,7 @@
         total = total + near_sum[k - 1]
     far_sum[far] = total
     copies = [tap_copy(far_sum.at[far], far_sum.at[far], far_to[k], near, 0) for k in range(1, group)]
-    loop(group - 2, group, leave(1))
+    loop(group - 2, group, leave(1)[1])
     for copy in copies:
         copy.wait()
     total = far_sum[0]
@@ -548,7 +599,8 @@
             for half in range(2):
                 seq_copy(k, p, half, 0, rows_here).wait_send()
     for m in range(size):
-        pltpu.make_async_copy(*bytes_of(m, out_ref.at[:, 0, pl.ds(0, tiles)]), in_send.at[m]).wait()
+        for half in range(2):
+            pltpu.make_async_copy(*in_bytes(m, half), in_send.at[m, half]).wait()
         for half, ref in enumerate((out_ref.at[:, :, 0], out_ref.at[:, :, pl.ds(0, tiles - 1)])):
             pltpu.make_async_copy(*bytes_of(m, ref), out_send.at[m, half]).wait()
             pltpu.make_async_copy(*bytes_of(m, ref), out_recv.at[m, half]).wait()
@@ -565,8 +617,8 @@
     slots = grad_in.shape[2]
     time_rows, width = rows_here * size, columns // 3 // size
     tiles = width // LANES
-    inner = -(-(time_rows + GAP * (SEGMENTS - 1)) // 96) * 96
-    rows_all = inner + 48 + 8
+    inner = -(-(time_rows + GAP * (SEGMENTS - 1)) // CONV) * CONV
+    rows_all = -(-(inner + 2 * GAP) // 48) * 48 + 8
     group = math.isqrt(data_size)
     piece = (group, (taps + 1) // group, width)
     sends = 2 * (group - 1) + group * size - 1
@@ -577,11 +629,13 @@
             jax.ShapeDtypeStruct((data_size, 3, size * tiles, slots, LANES), bf16),
             jax.ShapeDtypeStruct((taps, width * size), f32),
         ),
-        in_specs=[ANY, VMEM, pl.BlockSpec(memory_space=pltpu.SMEM), ANY, VMEM],
+        in_specs=[ANY, ANY, pl.BlockSpec(memory_space=pltpu.SMEM), ANY, ANY],
         out_specs=(ANY, VMEM),
         scratch_shapes=[
             pltpu.VMEM((size, 1, rows_here), seg.dtype),
             pltpu.VMEM((time_rows, 3 * width), bf16),
+            pltpu.VMEM((1, data_size, slots, size * width), bf16),
+            pltpu.VMEM(cw.shape, f32),
             pltpu.VMEM((data_size, slots, size * width), bf16),
             pltpu.VMEM((data_size * size, slots, width), bf16),
             pltpu.VMEM((data_size * size, 3, tiles, slots, LANES), bf16),
@@ -592,7 +646,7 @@
             pltpu.VMEM((rows_all, width), f32),
             pltpu.VMEM((width, time_rows), bf16),
             pltpu.VMEM((width, time_rows), bf16),
-            pltpu.VMEM((width, time_rows), f32),
+            pltpu.VMEM((width, time_rows), bf16),
             pltpu.VMEM((width, time_rows), f32),
             pltpu.VMEM((width, time_rows), f32),
             pltpu.VMEM((time_rows, width), f32),
@@ -603,11 +657,12 @@
             pltpu.VMEM(piece, f32),
             pltpu.VMEM(piece, f32),
             pltpu.VMEM((size,) + piece, f32),
-            dma((5,)),
+            pltpu.SemaphoreType.REGULAR,
+            dma((7,)),
             dma((size - 1, 7)),
             dma((size - 1, 7)),
-            dma((size,)),
-            dma((size,)),
+            dma((size, 2)),
+            dma((size, 2)),
             dma((size, 2)),
             dma((size, 2)),
             dma((sends,)),
@@ -622,6 +677,37 @@
     )(qkv, grad_in, counts, seg[None], cw)
 
 
+def hand_on_kernel(grads_ref, taps_ref, grads_out, taps_out, held, came, left):
+    pieces = came.shape[0]
+    count = held.shape[0] // pieces
+    here = [pl.ds(n * count, count) for n in range(pieces)]
+    reads = [pltpu.make_async_copy(grads_ref.at[h], held.at[h], came.at[n]) for n, h in enumerate(here)]
+    writes = [pltpu.make_async_copy(held.at[h], grads_out.at[h], left.at[n]) for n, h in enumerate(here)]
+    for copy in reads:
+        copy.start()
+    taps_out[...] = taps_ref[...]
+    for n in range(pieces):
+        reads[n].wait()
+        writes[n].start()
+    for copy in writes:
+        copy.wait()
+
+
+def hand_on(grads, total):
+    return pl.pallas_call(
+        hand_on_kernel,
+        out_shape=tuple(jax.ShapeDtypeStruct(x.shape, x.dtype) for x in (grads, total)),
+        in_specs=[ANY, VMEM],
+        out_specs=(ANY, VMEM),
+        scratch_shapes=[
+            pltpu.VMEM(grads.shape, grads.dtype),
+            pltpu.SemaphoreType.DMA((8,)),
+            pltpu.SemaphoreType.DMA((8,)),
+        ],
+        compiler_params=pltpu.CompilerParams(vmem_limit_bytes=60 * 1024 * 1024),
+    )(grads, total)
+
+
 def local(qkv, grad_in, counts, segment, conv_weight):
     data_size = lax.axis_size("dp")
     time_size = lax.axis_size("seq")
@@ -633,6 +719,7 @@
     grads, conv_weight_grad = run_block(
         qkv, grad_in, counts, segment, conv_weight, data_size, time_size, head_size, factor
     )
+    grads, conv_weight_grad = hand_on(grads, conv_weight_grad)
     qkv_grad = grads.transpose(0, 3, 1, 2, 4).reshape(1, data_size, slot_rows, 3 * width)
     return (qkv_grad, conv_weight_grad)
 

time: 120 us -> 116 us (0.967)
  local copies, waits for them, and re-layouts: 4.6 us -> 0 us
    unnamed x4 -> x0, local copies, waits for them, and re-layouts: 4.6 us -> none
    pallas_call x0 -> x1, Pallas kernels: none -> 4.1 us  [hand_on(): pl.pallas_call(hand_on_kernel, out_shape=tuple((jax.ShapeDtypeStruct(x.sh...]
    pallas_call x1, Pallas kernels: 115 us -> 111 us  [run_block(): pl.pallas_call(functools.partial(block_kernel, data_size, size, head_size...]
where the time goes in v6:
time: 116 us
  Pallas kernels  115 us (99%)
    pallas_call x1, Pallas kernels, run_block(): pl.pallas_call(functools.partial(block_kernel, data_size, size, head_size...  111 us
    pallas_call x1, Pallas kernels, hand_on(): pl.pallas_call(hand_on_kernel, out_shape=tuple((jax.ShapeDtypeStruct(x.sh...  4.1 us

profile of v6, /device:TPU:1, one launch (start us, length us, event | category | flops | bytes accessed | tf_op | source)
XLA Modules:
  0.0 116.0 jit_solution(5152581665334572474)
XLA Ops:
  0.6 111.2 %shard_map.68 = (bf16[64,3,12,4,128]{4,3,2,1,0:T(4,128)(2,1)}, f32[31,1536]{1,0:T(8,128)}) custom-call(bf16[1,256,4608]{2,1,0:T(8,128)(2,1)} %qkv_ref.1, bf16[1,64,4,1536]{3,2,1,0:T(4,128)(2,1)} %grad_in_ref.1, s32[1,64]{1,0:T(1,128)} %counts_ref.1, s32[1,1,256]{2,1,0:T(1,128)} %bitcast.5, f32[31,1536]{1,0:T(8,128)} %weights_ref.1), custom_call_target="tpu_custom_call" | custom-call | flops 5637144576 | bytes 67108864 | tf_op jit(solution)/shard_map/pallas_call | solution.py:626
  111.9 4.1 %shard_map.69 = (bf16[64,3,12,4,128]{4,3,2,1,0:T(4,128)(2,1)}, f32[31,1536]{1,0:T(8,128)}) custom-call(bf16[64,3,12,4,128]{4,3,2,1,0:T(4,128)(2,1)} %get-tuple-element.6.grads_ref, f32[31,1536]{1,0:T(8,128)} %get-tuple-element.7.taps_ref), custom_call_target="tpu_custom_call" | custom-call | tf_op jit(solution)/shard_map/pallas_call | solution.py:697

commit v7 on v6

--- a/solution.py
+++ b/solution.py
@@ -232,7 +232,7 @@
         lax.fori_loop(0, time_rows // UB, grad_step, 0, unroll=True)
         return carry
 
-    lax.fori_loop(0, time_rows // TB, time_block, 0)
+    lax.fori_loop(0, time_rows // TB, time_block, 0, unroll=True)
 
 
 def block_kernel(
@@ -242,7 +242,7 @@
     factor,
     qkv_ref,
     grad_in_ref,
-    counts_ref,
+    counts_in_ref,
     seg_ref,
     weights_ref,
     out_ref,
@@ -250,6 +250,7 @@
     seg_all,
     mine,
     grad_ref,
+    counts_ref,
     cw_ref,
     sent,
     cot,
@@ -347,6 +348,8 @@
     slot = me * data_size + data
     grad_copy = pltpu.make_async_copy(grad_in_ref, grad_ref, own_sem.at[5])
     grad_copy.start()
+    counts_copy = pltpu.make_async_copy(counts_in_ref, counts_ref, own_sem.at[7])
+    counts_copy.start()
     moves = [(seg_ref.at[0], seg_all.at[me])]
     for p in range(3):
         moves.append(
@@ -357,6 +360,7 @@
     for copy in own:
         copy.start()
     grad_copy.wait()
+    counts_copy.wait()
     slot_row = lax.broadcasted_iota(jnp.int32, sent.shape[1:], 0)
 
     def mark_empty(j):
@@ -629,12 +633,13 @@
             jax.ShapeDtypeStruct((data_size, 3, size * tiles, slots, LANES), bf16),
             jax.ShapeDtypeStruct((taps, width * size), f32),
         ),
-        in_specs=[ANY, ANY, pl.BlockSpec(memory_space=pltpu.SMEM), ANY, ANY],
+        in_specs=[pl.BlockSpec(memory_space=pltpu.HBM)] * 5,
         out_specs=(ANY, VMEM),
         scratch_shapes=[
             pltpu.VMEM((size, 1, rows_here), seg.dtype),
             pltpu.VMEM((time_rows, 3 * width), bf16),
             pltpu.VMEM((1, data_size, slots, size * width), bf16),
+            pltpu.SMEM(counts.shape, counts.dtype),
             pltpu.VMEM(cw.shape, f32),
             pltpu.VMEM((data_size, slots, size * width), bf16),
             pltpu.VMEM((data_size * size, slots, width), bf16),
@@ -658,7 +663,7 @@
             pltpu.VMEM(piece, f32),
             pltpu.VMEM((size,) + piece, f32),
             pltpu.SemaphoreType.REGULAR,
-            dma((7,)),
+            dma((8,)),
             dma((size - 1, 7)),
             dma((size - 1, 7)),
             dma((size, 2)),
@@ -669,43 +674,12 @@
             dma((sends,)),
         ],
         compiler_params=pltpu.CompilerParams(
-            collective_id=1, has_side_effects=True, vmem_limit_bytes=58 * 1024 * 1024
+            collective_id=1, has_side_effects=True, vmem_limit_bytes=50 * 1024 * 1024
         ),
         cost_estimate=pl.CostEstimate(
             flops=14 * time_rows * time_rows * width, bytes_accessed=64 << 20, transcendentals=0
         ),
     )(qkv, grad_in, counts, seg[None], cw)
-
-
-def hand_on_kernel(grads_ref, taps_ref, grads_out, taps_out, held, came, left):
-    pieces = came.shape[0]
-    count = held.shape[0] // pieces
-    here = [pl.ds(n * count, count) for n in range(pieces)]
-    reads = [pltpu.make_async_copy(grads_ref.at[h], held.at[h], came.at[n]) for n, h in enumerate(here)]
-    writes = [pltpu.make_async_copy(held.at[h], grads_out.at[h], left.at[n]) for n, h in enumerate(here)]
-    for copy in reads:
-        copy.start()
-    taps_out[...] = taps_ref[...]
-    for n in range(pieces):
-        reads[n].wait()
-        writes[n].start()
-    for copy in writes:
-        copy.wait()
-
-
-def hand_on(grads, total):
-    return pl.pallas_call(
-        hand_on_kernel,
-        out_shape=tuple(jax.ShapeDtypeStruct(x.shape, x.dtype) for x in (grads, total)),
-        in_specs=[ANY, VMEM],
-        out_specs=(ANY, VMEM),
-        scratch_shapes=[
-            pltpu.VMEM(grads.shape, grads.dtype),
-            pltpu.SemaphoreType.DMA((8,)),
-            pltpu.SemaphoreType.DMA((8,)),
-        ],
-        compiler_params=pltpu.CompilerParams(vmem_limit_bytes=60 * 1024 * 1024),
-    )(grads, total)
 
 
 def local(qkv, grad_in, counts, segment, conv_weight):
@@ -719,7 +693,6 @@
     grads, conv_weight_grad = run_block(
         qkv, grad_in, counts, segment, conv_weight, data_size, time_size, head_size, factor
     )
-    grads, conv_weight_grad = hand_on(grads, conv_weight_grad)
     qkv_grad = grads.transpose(0, 3, 1, 2, 4).reshape(1, data_size, slot_rows, 3 * width)
     return (qkv_grad, conv_weight_grad)
 

time: 116 us -> 115 us (level)
  Pallas kernels: 115 us -> 108 us
  local copies, waits for them, and re-layouts: 0 us -> 5.47 us
    unnamed x0 -> x10, local copies, waits for them, and re-layouts: none -> 5.47 us
    pallas_call x1 -> x0, Pallas kernels: 4.1 us -> none  [hand_on(): pl.pallas_call(hand_on_kernel, out_shape=tuple((jax.ShapeDtypeStruct(x.sh...]
    pallas_call x1, Pallas kernels: 111 us -> 108 us  [run_block(): pl.pallas_call(functools.partial(block_kernel, data_size, size, head_size...]
where the time goes in v7:
time: 115 us; the launch traced here: 114 us
  Pallas kernels  108 us (94%)
  local copies, waits for them, and re-layouts  5.47 us (5%)
    pallas_call x1, Pallas kernels, run_block(): pl.pallas_call(functools.partial(block_kernel, data_size, size, head_size...  108 us
    unnamed x10, local copies, waits for them, and re-layouts  5.47 us

profile of v7, /device:TPU:1, one launch (start us, length us, event | category | flops | bytes accessed | tf_op | source)
XLA Modules:
  0.0 114.4 jit_solution(10063267883277119812)
XLA Ops:
  0.6 0.0 copy-start
  0.6 1.1 copy-done
  1.8 0.0 copy-start.1
  1.8 0.9 copy-done.1
  2.7 0.0 copy-start.2
  2.7 0.7 copy-done.2
  3.4 0.0 copy-start.3
  3.4 0.7 copy-done.3
  4.0 108.2 %shard_map.68 = (bf16[64,3,12,4,128]{4,3,2,1,0:T(4,128)(2,1)S(1)}, f32[31,1536]{1,0:T(8,128)S(1)}) custom-call(bf16[1,256,4608]{2,1,0:T(8,128)(2,1)} %qkv_ref.1, bf16[1,64,4,1536]{3,2,1,0:T(4,128)(2,1)S(1)} %copy-done, s32[1,64]{1,0:T(1,128)S(1)} %copy-done.3, s32[1,1,256]{2,1,0:T(1,128)S(1)} %bitcast.5, f32[31,1536]{1,0:T(8,128)S(1)} %copy-done.1), custom_call_target="tpu_custom_call" | custom-call | flops 5637144576 | bytes 67108864 | tf_op jit(solution)/shard_map/pallas_call | solution.py:630
  112.3 1.4 %copy.9 = bf16[1,64,4,4608]{3,2,1,0:T(4,128)(2,1)} copy(bf16[1,64,4,4608]{3,2,1,0:T(4,128)(2,1)S(1)} %bitcast.4) | data formatting | bytes 4718592
  113.7 0.7 copy.10
Async XLA Ops:
  0.6 1.1 copy-start
  1.8 0.9 copy-start.1
  2.7 0.7 copy-start.2
  3.4 0.7 copy-start.3

commit v8 on v7

--- a/solution.py
+++ b/solution.py
@@ -359,21 +359,6 @@
     own = [pltpu.make_async_copy(src, dst, own_sem.at[n]) for n, (src, dst) in enumerate(moves)]
     for copy in own:
         copy.start()
-    grad_copy.wait()
-    counts_copy.wait()
-    slot_row = lax.broadcasted_iota(jnp.int32, sent.shape[1:], 0)
-
-    def mark_empty(j):
-        val = jnp.where(slot_row < counts_ref[0, j], grad_ref[0, j].astype(f32), EMPTY)
-        sent[j] = val.astype(bf16)
-
-    chunks(data_size, mark_empty)
-    own_cot = pltpu.make_async_copy(sent.at[data, :, part_cols(0, me)], cot.at[slot], own_sem.at[6])
-    own_cot.start()
-    clear(shifted.at[0])
-    clear(att_pad)
-    clear(dk)
-    clear(dv)
     pl.semaphore_wait(barrier_sem, group - 1 + len(across))
     for z, m in across:
         pl.semaphore_signal(
@@ -382,7 +367,17 @@
             device_id={"dp": lax.rem(far + z, group) * group + near, "seq": to[m]},
             device_id_type=MESH,
         )
-
+    grad_copy.wait()
+    counts_copy.wait()
+    slot_row = lax.broadcasted_iota(jnp.int32, sent.shape[1:], 0)
+
+    def mark_empty(j):
+        val = jnp.where(slot_row < counts_ref[0, j], grad_ref[0, j].astype(f32), EMPTY)
+        sent[j] = val.astype(bf16)
+
+    chunks(data_size, mark_empty)
+    own_cot = pltpu.make_async_copy(sent.at[data, :, part_cols(0, me)], cot.at[slot], own_sem.at[6])
+    own_cot.start()
     halves = ((0, 2 * LANES), (2 * LANES, part - 2 * LANES))
 
     def seg_copy(k):
@@ -442,6 +437,10 @@
     for p in range(3):
         for k in range(1, size):
             seq_copy(k, p, 0, early, rows_here - early).start()
+    clear(shifted.at[0])
+    clear(att_pad)
+    clear(dk)
+    clear(dv)
 
     def bytes_of(m, ref):
         got = ref.at[pl.ds(0, data_size if m else data_size - 1)]

time: 115 us -> 114 us (level)
  no operation moved by 1% of the time
where the time goes in v8:
time: 114 us
  Pallas kernels  108 us (95%)
  local copies, waits for them, and re-layouts  5.47 us (5%)
    pallas_call x1, Pallas kernels, run_block(): pl.pallas_call(functools.partial(block_kernel, data_size, size, head_size...  108 us
    unnamed x10, local copies, waits for them, and re-layouts  5.47 us

profile of v8, /device:TPU:1, one launch (start us, length us, event | category | flops | bytes accessed | tf_op | source)
XLA Modules:
  0.0 113.7 jit_solution(14992654638807096390)
XLA Ops:
  0.6 0.0 copy-start
  0.6 1.1 copy-done
  1.8 0.0 copy-start.1
  1.8 0.9 copy-done.1
  2.7 0.0 copy-start.2
  2.7 0.7 copy-done.2
  3.4 0.0 copy-start.3
  3.4 0.7 copy-done.3
  4.0 107.5 %shard_map.68 = (bf16[64,3,12,4,128]{4,3,2,1,0:T(4,128)(2,1)S(1)}, f32[31,1536]{1,0:T(8,128)S(1)}) custom-call(bf16[1,256,4608]{2,1,0:T(8,128)(2,1)} %qkv_ref.1, bf16[1,64,4,1536]{3,2,1,0:T(4,128)(2,1)S(1)} %copy-done, s32[1,64]{1,0:T(1,128)S(1)} %copy-done.3, s32[1,1,256]{2,1,0:T(1,128)S(1)} %bitcast.5, f32[31,1536]{1,0:T(8,128)S(1)} %copy-done.1), custom_call_target="tpu_custom_call" | custom-call | flops 5637144576 | bytes 67108864 | tf_op jit(solution)/shard_map/pallas_call | solution.py:629
  111.6 1.4 %copy.9 = bf16[1,64,4,4608]{3,2,1,0:T(4,128)(2,1)} copy(bf16[1,64,4,4608]{3,2,1,0:T(4,128)(2,1)S(1)} %bitcast.4) | data formatting | bytes 4718592
  113.0 0.7 copy.10
Async XLA Ops:
  0.6 1.1 copy-start
  1.8 0.9 copy-start.1
  2.7 0.7 copy-start.2
  3.4 0.7 copy-start.3
